TPU v7x, 128 devices: a whole 4x4x4 slice. The times are simulated.
128 devices in a mesh: row: 32 (over y_hi, z, x), col: 4 (over y_lo, core).
Axes of the slice: x: 4, y: 4 (y_hi: 2, y_lo: 2; y = y_hi * 2 + y_lo), z: 4, core: 2. Of those that a mesh axis runs over, the one named last changes fastest.
Arguments:
- layer_input: bfloat16 [16384, 1088], P('row', 'col'), may hold values from -32 to 32
- first_norm_gain: float32 [1088], P('col'), may hold values from 0.5 to 1.5
- first_norm_bias: float32 [1088], P('col'), may hold values from -1.5 to 1.5
- w_qkv: bfloat16 [1088, 3264], P('row', 'col'), may hold values from -0.7276069 to 0.7276069
- w_out: bfloat16 [1088, 1088], P('col', 'row'), may hold values from -3 to 3
- second_norm_gain: float32 [1088], P('col'), may hold values from 0.5 to 1.5
- second_norm_bias: float32 [1088], P('col'), may hold values from -1.5 to 1.5
- w_up: bfloat16 [1088, 4352], P('row', 'col'), may hold values from -0.1875 to 0.1875
- w_down: bfloat16 [4352, 1088], P('col', 'row'), may hold values from -0.09375 to 0.09375
- gradient_of_output: bfloat16 [16384, 1088], P('row', 'col'), may hold values from -6 to 6
Outputs:
- layer_output: bfloat16 [16384, 1088], P('row', 'col')
- gradient_of_input: float32 [16384, 1088], P('row', 'col')
- first_gain_gradient: float32 [1088], P('col')
- grad_norm1_bias: float32 [1088], P('col')
- grad_w_qkv: float32 [1088, 3264], P('row', 'col')
- grad_w_out: float32 [1088, 1088], P('col', 'row')
- second_gain_gradient: float32 [1088], P('col')
- grad_norm2_bias: float32 [1088], P('col')
- grad_w_up: float32 [1088, 4352], P('row', 'col')
- grad_w_down: float32 [4352, 1088], P('col', 'row')
All inputs are finite; a program needn't handle non-finite values.
Results may differ from a plain program's by a relative error of at most 0.025.
Values may be sent and summed in bfloat16 or wider, within the bound.
A program may use at most 128 MiB of HBM per device.

v0:
```python
import math

import jax
import jax.numpy as jnp
from jax import lax
from jax.sharding import PartitionSpec as P

HEADS = 17
HEAD_DIM = 64
D = 1088
SEQ = 2048


gelu_coef = math.sqrt(2.0 / math.pi)
norm_epsilon = 1e-05
masked_score = -1e30


def from_behind(block, axis, distance):
    devices = range(lax.axis_size(axis))
    route = [(i - distance, i) for i in devices if i - distance in devices]
    return lax.ppermute(block, axis, route)


def gelu_value(values):
    tanh_input = gelu_coef * (values + 0.044715 * values * values * values)
    return 0.5 * values * (1.0 + jnp.tanh(tanh_input))


def gelu_slope(values):
    tanh_input = gelu_coef * (values + 0.044715 * values * values * values)
    tanh_value = jnp.tanh(tanh_input)
    return 0.5 * (1.0 + tanh_value) + 0.5 * values * (1.0 - tanh_value * tanh_value) * gelu_coef * (
        1.0 + 0.134145 * values * values
    )


def feature_sums(first_sum, second_sum):
    return lax.psum((first_sum, second_sum), "col")


def spread_rows(piece):
    return lax.all_gather(piece, "col", axis=1, tiled=True)


def feature_total(partial_value):
    return lax.psum_scatter(
        partial_value.astype(jnp.bfloat16), "col", scatter_dimension=1, tiled=True
    ).astype(jnp.float32)


def to_queries(piece):
    return lax.all_to_all(piece, "col", split_axis=0, concat_axis=1, tiled=True)


def to_tokens(piece):
    return lax.all_to_all(piece, "col", split_axis=1, concat_axis=0, tiled=True)


def layernorm_apply(value_rows, gain_row, bias_row):
    total_sum, square_sum = feature_sums(
        jnp.sum(value_rows, axis=1), jnp.sum(value_rows * value_rows, axis=1)
    )
    mean_value = (total_sum / D)[:, None]
    inverse_std = lax.rsqrt((square_sum / D)[:, None] - mean_value * mean_value + norm_epsilon)
    normed = (value_rows - mean_value) * inverse_std
    return (normed, inverse_std, (normed * gain_row + bias_row).astype(jnp.bfloat16))


def layernorm_reverse(grad_rows, normed, inverse_std, gain_row):
    scaled = grad_rows * gain_row
    first_sum, second_sum = feature_sums(jnp.sum(scaled, axis=1), jnp.sum(scaled * normed, axis=1))
    return inverse_std * (scaled - (first_sum / D)[:, None] - normed * (second_sum / D)[:, None])


def piece_scores(query_heads, piece, query_pos, piece_start, seq_start):
    key_heads = piece[:, :D].reshape(piece.shape[0], HEADS, HEAD_DIM)
    scores = jnp.einsum(
        "qhe,khe->hqk", query_heads, key_heads, preferred_element_type=jnp.float32
    ) * HEAD_DIM ** (-0.5)
    key_pos = piece_start + jnp.arange(piece.shape[0], dtype=jnp.int32)
    allowed = ((key_pos[None, :] <= query_pos[:, None]) & (key_pos[None, :] >= seq_start))[None]
    return (scores, allowed)


def per_device(
    layer_input,
    first_norm_gain,
    first_norm_bias,
    w_qkv,
    w_out,
    second_norm_gain,
    second_norm_bias,
    w_up,
    w_down,
    gradient_of_output,
):
    tokens_here = layer_input.shape[0]
    quarter_rows = tokens_here // lax.axis_size("col")
    col_index = lax.axis_index("col")
    row_index = lax.axis_index("row")
    chain_length = SEQ // tokens_here
    qkv_weight, up_weight, out_weight, down_weight = (
        lax.all_gather(w_qkv, "row", axis=0, tiled=True),
        lax.all_gather(w_up, "row", axis=0, tiled=True),
        lax.all_gather(w_out, "row", axis=1, tiled=True),
        lax.all_gather(w_down, "row", axis=1, tiled=True),
    )
    sender_block = layer_input.astype(jnp.float32)
    first_centered_input, first_reciprocal_deviation, first_norm_slice = layernorm_apply(
        sender_block, first_norm_gain, first_norm_bias
    )
    norm1_full = spread_rows(first_norm_slice)
    qkv_local = jnp.dot(norm1_full, qkv_weight, preferred_element_type=jnp.float32).astype(
        jnp.bfloat16
    )
    grouped = to_queries(qkv_local)
    query_rows = grouped[:, :D]
    kv_pairs = lax.all_gather(grouped[:, D:], "col", axis=0, tiled=True)
    query_heads = query_rows.reshape(quarter_rows, HEADS, HEAD_DIM)
    pieces = [kv_pairs]
    for piece_index in range(1, chain_length):
        pieces.append(from_behind(pieces[-1], "row", 1))
    query_pos = (
        row_index * tokens_here
        + col_index * quarter_rows
        + jnp.arange(quarter_rows, dtype=jnp.int32)
    )
    seq_start = jnp.maximum((row_index * tokens_here + SEQ // 2) // SEQ * SEQ - SEQ // 2, 0)
    peak = jnp.full((HEADS, quarter_rows, 1), masked_score, jnp.float32)
    running = jnp.zeros((HEADS, quarter_rows, 1), jnp.float32)
    kept_scores = []
    for piece_index in range(chain_length):
        scores, allowed = piece_scores(
            query_heads,
            pieces[piece_index],
            query_pos,
            (row_index - piece_index) * tokens_here,
            seq_start,
        )
        kept_scores.append((scores, allowed))
        masked = jnp.where(allowed, scores, masked_score)
        new_peak = jnp.maximum(peak, jnp.max(masked, axis=2, keepdims=True))
        running = running * jnp.exp(peak - new_peak) + jnp.sum(
            jnp.where(allowed, jnp.exp(masked - new_peak), 0.0), axis=2, keepdims=True
        )
        peak = new_peak
    log_total = peak + jnp.log(running)
    mixed_sum = jnp.zeros((quarter_rows, HEADS, HEAD_DIM), jnp.float32)
    for piece_index in range(chain_length):
        scores, allowed = kept_scores[piece_index]
        probs = jnp.where(allowed, jnp.exp(scores - log_total), 0.0).astype(jnp.bfloat16)
        value_heads = pieces[piece_index][:, D:].reshape(tokens_here, HEADS, HEAD_DIM)
        mixed_sum = mixed_sum + jnp.einsum(
            "hqk,khe->qhe", probs, value_heads, preferred_element_type=jnp.float32
        )
    attn_query = mixed_sum.reshape(quarter_rows, D).astype(jnp.bfloat16)
    attn_local = to_tokens(attn_query)
    residual_stream = sender_block + feature_total(
        jnp.dot(attn_local, out_weight, preferred_element_type=jnp.float32)
    )
    second_centered_input, second_reciprocal_deviation, second_norm_slice = layernorm_apply(
        residual_stream, second_norm_gain, second_norm_bias
    )
    norm2_full = spread_rows(second_norm_slice)
    pre = jnp.dot(norm2_full, up_weight, preferred_element_type=jnp.float32)
    hidden = gelu_value(pre).astype(jnp.bfloat16)
    layer_output = (
        residual_stream
        + feature_total(jnp.dot(hidden, down_weight, preferred_element_type=jnp.float32))
    ).astype(jnp.bfloat16)
    cot_full = spread_rows(gradient_of_output)
    d_hidden = jnp.dot(cot_full, down_weight.T, preferred_element_type=jnp.float32)
    d_pre = (d_hidden * gelu_slope(pre)).astype(jnp.bfloat16)
    part_down = jnp.dot(hidden.T, cot_full, preferred_element_type=jnp.float32)
    part_up = jnp.dot(norm2_full.T, d_pre, preferred_element_type=jnp.float32)
    second_norm_gradient = feature_total(
        jnp.dot(d_pre, up_weight.T, preferred_element_type=jnp.float32)
    )
    second_gain_portion = jnp.sum(second_norm_gradient * second_centered_input, axis=0)
    bias2_part = jnp.sum(second_norm_gradient, axis=0)
    residual_gradient = gradient_of_output.astype(jnp.float32) + layernorm_reverse(
        second_norm_gradient, second_centered_input, second_reciprocal_deviation, second_norm_gain
    )
    resid_full = spread_rows(residual_gradient.astype(jnp.bfloat16))
    part_out = jnp.dot(attn_local.T, resid_full, preferred_element_type=jnp.float32)
    d_mix_local = jnp.dot(resid_full, out_weight.T, preferred_element_type=jnp.float32).astype(
        jnp.bfloat16
    )
    d_mix_heads = to_queries(d_mix_local).reshape(quarter_rows, HEADS, HEAD_DIM)
    attn_heads = attn_query.reshape(quarter_rows, HEADS, HEAD_DIM)
    delta = jnp.einsum(
        "qhe,qhe->hq", d_mix_heads.astype(jnp.float32), attn_heads.astype(jnp.float32)
    )[:, :, None]

    def piece_grads(piece_index):
        piece = pieces[piece_index]
        scores, allowed = piece_scores(
            query_heads, piece, query_pos, (row_index - piece_index) * tokens_here, seq_start
        )
        probs = jnp.where(allowed, jnp.exp(scores - log_total), 0.0).astype(jnp.bfloat16)
        key_heads = piece[:, :D].reshape(tokens_here, HEADS, HEAD_DIM)
        value_heads = piece[:, D:].reshape(tokens_here, HEADS, HEAD_DIM)
        d_value = jnp.einsum("hqk,qhe->khe", probs, d_mix_heads, preferred_element_type=jnp.float32)
        d_prob = jnp.einsum(
            "qhe,khe->hqk", d_mix_heads, value_heads, preferred_element_type=jnp.float32
        )
        d_scores = (probs.astype(jnp.float32) * (d_prob - delta)).astype(jnp.bfloat16)
        query_term = jnp.einsum(
            "hqk,khe->qhe", d_scores, key_heads, preferred_element_type=jnp.float32
        ) * HEAD_DIM ** (-0.5)
        d_key = jnp.einsum(
            "hqk,qhe->khe", d_scores, query_heads, preferred_element_type=jnp.float32
        ) * HEAD_DIM ** (-0.5)
        joined = jnp.concatenate(
            [d_key.reshape(tokens_here, D), d_value.reshape(tokens_here, D)], axis=1
        )
        return (joined, query_term)

    carried, d_query = piece_grads(chain_length - 1)
    for piece_index in range(chain_length - 2, -1, -1):
        joined, query_term = piece_grads(piece_index)
        carried = (
            from_behind(carried.astype(jnp.bfloat16), "row", -1).astype(carried.dtype) + joined
        )
        d_query = d_query + query_term
    d_query_rows = d_query.reshape(quarter_rows, D)
    kv_summed = lax.psum_scatter(
        carried.astype(jnp.bfloat16), "col", scatter_dimension=0, tiled=True
    ).astype(jnp.float32)
    d_qkv = to_tokens(jnp.concatenate([d_query_rows, kv_summed], axis=1).astype(jnp.bfloat16))
    part_qkv = jnp.dot(norm1_full.T, d_qkv, preferred_element_type=jnp.float32)
    first_norm_gradient = feature_total(
        jnp.dot(d_qkv, qkv_weight.T, preferred_element_type=jnp.float32)
    )
    first_gain_portion = jnp.sum(first_norm_gradient * first_centered_input, axis=0)
    bias1_part = jnp.sum(first_norm_gradient, axis=0)
    gradient_of_input = residual_gradient + layernorm_reverse(
        first_norm_gradient, first_centered_input, first_reciprocal_deviation, first_norm_gain
    )
    grad_qkv, grad_up, grad_out, grad_down = (
        lax.psum_scatter(
            part_qkv.astype(jnp.bfloat16), "row", scatter_dimension=0, tiled=True
        ).astype(jnp.float32),
        lax.psum_scatter(
            part_up.astype(jnp.bfloat16), "row", scatter_dimension=0, tiled=True
        ).astype(jnp.float32),
        lax.psum_scatter(
            part_out.astype(jnp.bfloat16), "row", scatter_dimension=1, tiled=True
        ).astype(jnp.float32),
        lax.psum_scatter(
            part_down.astype(jnp.bfloat16), "row", scatter_dimension=1, tiled=True
        ).astype(jnp.float32),
    )
    gain1_grad, bias1_grad, gain2_grad, bias2_grad = lax.psum(
        (first_gain_portion, bias1_part, second_gain_portion, bias2_part), "row"
    )
    return (
        layer_output,
        gradient_of_input,
        gain1_grad,
        bias1_grad,
        grad_qkv,
        grad_out,
        gain2_grad,
        bias2_grad,
        grad_up,
        grad_down,
    )


def solution(mesh):
    placed = (
        P("row", "col"),
        P("col"),
        P("col"),
        P("row", "col"),
        P("col", "row"),
        P("col"),
        P("col"),
        P("row", "col"),
        P("col", "row"),
        P("row", "col"),
    )
    return jax.shard_map(
        per_device,
        mesh=mesh,
        in_specs=placed,
        out_specs=(
            P("row", "col"),
            P("row", "col"),
            P("col"),
            P("col"),
            P("row", "col"),
            P("col", "row"),
            P("col"),
            P("col"),
            P("row", "col"),
            P("col", "row"),
        ),
        check_vma=False,
    )
```

profile of v0, /device:TPU:1, one launch (start us, length us, event | category | flops | bytes accessed | tf_op | source)
XLA Modules:
  0.0 1413.7 jit_solution(5524050979346493890)
XLA Ops:
  9.0 6.5 all-reduce.12
  17.4 67.1 %all-gather.23.cloned.1.call-done = bf16[32,34,816]{2,1,0:T(8,128)(2,1)} async-done(((bf16[1,34,816]{2,1,0:T(8,128)(2,1)}), bf16[32,34,816]{2,1,0:T(8,128)(2,1)}) %all-gather.23.cloned.1.call-update) | async-done | bytes 1775632 | tf_op jit(solution)/shard_map/all_gather | solution.py:104
  87.4 19.3 %all-gather.13.cloned.1.call-done = bf16[512,1088]{0,1:T(8,128)(2,1)} async-done(((bf16[512,272]{0,1:T(8,128)(2,1)}), bf16[512,1088]{0,1:T(8,128)(2,1)}) %all-gather.13.cloned.1.call-update) | async-done | bytes 1114128 | tf_op jit(solution)/shard_map/all_gather | solution.py:43
  109.4 14.2 %all_to_all.67 = bf16[4,128,816]{1,2,0:T(8,128)(2,1)S(1)} all-to-all(bf16[4,128,816]{1,2,0:T(8,128)(2,1)S(1)} %bitcast.216), channel_id=1, replica_groups=mesh['row'=32,'col'=4] {'col'}, dimensions={0} | all-to-all | bytes 1671168 | tf_op jit(solution)/shard_map/all_to_all | solution.py:53
  124.4 31.6 %all-gather.15.cloned.1.call-done = bf16[512,2176]{0,1:T(8,128)(2,1)} async-done(((bf16[128,2176]{0,1:T(8,128)(2,1)}), bf16[512,2176]{0,1:T(8,128)(2,1)}) %all-gather.15.cloned.1.call-update) | async-done | bytes 2228240 | tf_op jit(solution)/shard_map/all_gather | solution.py:119
  160.5 46.6 %collective-permute-done = bf16[512,2176]{0,1:T(8,128)(2,1)} collective-permute-done((bf16[512,2176]{0,1:T(8,128)(2,1)}, bf16[512,2176]{0,1:T(8,128)(2,1)}, u32[]{:S(2)}, u32[]{:S(2)}) %collective-permute-start) | collective-permute-done | bytes 2228256 | tf_op jit(solution)/shard_map/ppermute | solution.py:22
  214.3 44.6 %collective-permute-done.1 = bf16[512,2176]{0,1:T(8,128)(2,1)} collective-permute-done((bf16[512,2176]{0,1:T(8,128)(2,1)}, bf16[512,2176]{0,1:T(8,128)(2,1)}, u32[]{:S(2)}, u32[]{:S(2)}) %collective-permute-start.1) | collective-permute-done | bytes 2228256 | tf_op jit(solution)/shard_map/ppermute | solution.py:22
  272.1 37.9 %collective-permute-done.2 = bf16[512,2176]{0,1:T(8,128)(2,1)S(1)} collective-permute-done((bf16[512,2176]{0,1:T(8,128)(2,1)}, bf16[512,2176]{0,1:T(8,128)(2,1)S(1)}, u32[]{:S(2)}, u32[]{:S(2)}) %collective-permute-start.2) | collective-permute-done | bytes 2228256 | tf_op jit(solution)/shard_map/ppermute | solution.py:22
  335.5 91.8 %all-gather.1 = bf16[32,34,272]{2,1,0:T(8,128)(2,1)} all-gather(bf16[1,34,272]{2,1,0:T(8,128)(2,1)S(1)} %bitcast.222), channel_id=1, replica_groups=mesh['row'=32,'col'=4] {'row'}, dimensions={0}, use_global_device_ids=true | all-gather | bytes 610368 | tf_op jit(solution)/shard_map/all_gather | solution.py:106
  433.9 41.2 %reduce-scatter.16.cloned.1.call-done = bf16[512,272]{0,1:T(8,128)(2,1)} async-done(((bf16[512,1088]{0,1:T(8,128)(2,1)}), bf16[512,272]{0,1:T(8,128)(2,1)}) %reduce-scatter.16.cloned.1.call-update) | async-done | bytes 278544 | tf_op jit(solution)/shard_map/reduce_scatter | solution.py:47
  484.3 68.0 %all-gather.25.cloned.1.call-done = bf16[32,34,1088]{2,1,0:T(8,128)(2,1)} async-done(((bf16[1,34,1088]{2,1,0:T(8,128)(2,1)}), bf16[32,34,1088]{2,1,0:T(8,128)(2,1)}) %all-gather.25.cloned.1.call-update) | async-done | bytes 2367504 | tf_op jit(solution)/shard_map/all_gather | solution.py:105
  556.8 70.2 %all-gather.27.cloned.1.call-done = bf16[32,34,1088]{2,1,0:T(8,128)(2,1)} async-done(((bf16[1,34,1088]{2,1,0:T(8,128)(2,1)}), bf16[32,34,1088]{2,1,0:T(8,128)(2,1)}) %all-gather.27.cloned.1.call-update) | async-done | bytes 2367504 | tf_op jit(solution)/shard_map/all_gather | solution.py:107
  631.5 17.5 %all-gather.17.cloned.1.call-done = bf16[512,1088]{0,1:T(8,128)(2,1)} async-done(((bf16[512,272]{0,1:T(8,128)(2,1)}), bf16[512,1088]{0,1:T(8,128)(2,1)}) %all-gather.17.cloned.1.call-update) | async-done | bytes 1114128 | tf_op jit(solution)/shard_map/all_gather | solution.py:43
  654.1 18.7 %all-gather.19.cloned.1.call-done = bf16[512,1088]{0,1:T(8,128)(2,1)} async-done(((bf16[512,272]{0,1:T(8,128)(2,1)}), bf16[512,1088]{0,1:T(8,128)(2,1)}) %all-gather.19.cloned.1.call-update) | async-done | bytes 1114128 | tf_op jit(solution)/shard_map/all_gather | solution.py:43
  672.8 5.6 fusion.7
  682.1 21.5 %reduce-scatter.20.cloned.1.call-done = bf16[512,272]{0,1:T(8,128)(2,1)} async-done(((bf16[512,1088]{0,1:T(8,128)(2,1)}), bf16[512,272]{0,1:T(8,128)(2,1)}) %reduce-scatter.20.cloned.1.call-update) | async-done | bytes 278544 | tf_op jit(solution)/shard_map/reduce_scatter | solution.py:47
  713.1 23.1 %all-gather.21.cloned.1.call-done = bf16[512,1088]{0,1:T(8,128)(2,1)} async-done(((bf16[512,272]{0,1:T(8,128)(2,1)}), bf16[512,1088]{0,1:T(8,128)(2,1)}) %all-gather.21.cloned.1.call-update) | async-done | bytes 1114128 | tf_op jit(solution)/shard_map/all_gather | solution.py:43
  738.5 8.3 all_to_all.68
  755.4 47.3 %collective-permute-done.3 = bf16[512,2176]{0,1:T(8,128)(2,1)S(1)} collective-permute-done((bf16[512,2176]{0,1:T(8,128)(2,1)S(1)}, bf16[512,2176]{0,1:T(8,128)(2,1)S(1)}, u32[]{:S(2)}, u32[]{:S(2)}) %collective-permute-start.3) | collective-permute-done | bytes 2228256 | tf_op jit(solution)/shard_map/ppermute | solution.py:22
  807.7 46.4 %collective-permute-done.4 = bf16[512,2176]{0,1:T(8,128)(2,1)S(1)} collective-permute-done((bf16[512,2176]{0,1:T(8,128)(2,1)S(1)}, bf16[512,2176]{0,1:T(8,128)(2,1)S(1)}, u32[]{:S(2)}, u32[]{:S(2)}) %collective-permute-start.4) | collective-permute-done | bytes 2228256 | tf_op jit(solution)/shard_map/ppermute | solution.py:22
  859.1 45.5 %collective-permute-done.5 = bf16[512,2176]{0,1:T(8,128)(2,1)S(1)} collective-permute-done((bf16[512,2176]{0,1:T(8,128)(2,1)S(1)}, bf16[512,2176]{0,1:T(8,128)(2,1)S(1)}, u32[]{:S(2)}, u32[]{:S(2)}) %collective-permute-start.5) | collective-permute-done | bytes 2228256 | tf_op jit(solution)/shard_map/ppermute | solution.py:22
  916.7 39.1 %reduce-scatter.24.cloned.1.call-done = bf16[128,2176]{1,0:T(8,128)(2,1)} async-done(((bf16[512,2176]{1,0:T(8,128)(2,1)}), bf16[128,2176]{1,0:T(8,128)(2,1)}) %reduce-scatter.24.cloned.1.call-update) | async-done | bytes 557072
  957.2 14.3 %all_to_all.69 = bf16[128,4,816]{0,2,1:T(8,128)(2,1)S(1)} all-to-all(bf16[128,4,816]{0,2,1:T(8,128)(2,1)S(1)} %bitcast.215), channel_id=1, replica_groups=mesh['row'=32,'col'=4] {'col'}, dimensions={1} | all-to-all | bytes 1671168 | tf_op jit(solution)/shard_map/all_to_all | solution.py:57
  991.9 131.0 %fusion.54 = (bf16[48,816]{1,0:T(8,128)(2,1)S(1)}, bf16[272,48]{0,1:T(8,128)(2,1)}, bf16[48,1088]{1,0:T(8,128)(2,1)S(1)}, bf16[1088,48]{0,1:T(8,128)(2,1)}) fusion(bf16[1088,816]{1,0:T(8,128)(2,1)} %convolution_convert_fusion.2, bf16[272,1088]{0,1:T(8,128)(2,1)} %convolution_convert_fusion.7, bf16[1088,1088]{1,0:T(8,128)(2,1)S(1)} %convolution_convert_fusion.1, ...), kind=kCustom, calls=%all-reduce-scatter.4 | all-reduce-scatter fusion | flops 5013505 | bytes 7416320
  1127.0 11.6 collective-permute-start.15
  1142.0 7.5 collective-permute-start.45
  1199.0 6.1 collective-permute-start.38
  1243.8 8.1 concatenate.22
  1263.4 5.9 concatenate.25
  1269.4 16.4 %concatenate.24 = bf16[482,1088]{1,0:T(8,128)(2,1)} concatenate(bf16[2,1088]{1,0:T(2,128)(2,1)S(1)} %collective-permute-done.35, bf16[48,1088]{1,0:T(8,128)(2,1)} %collective-permute-done.34, bf16[48,1088]{1,0:T(8,128)(2,1)} %collective-permute-done.33, bf16[48,1088]{1,0:T(8,128)(2,1)} %collective-permute-done.32, bf16[48,1088]{1,0:T(8,128)(2,1)} %collective-permute-done.31, ...), dimensions={0} | concatenate | bytes 2097664
  1289.4 77.1 %all-reduce.8 = (f32[272]{0:T(512)}, f32[272]{0:T(512)}, f32[272]{0:T(512)}, f32[272]{0:T(512)}) all-reduce(f32[272]{0:T(512)S(1)} %get-tuple-element.12, f32[272]{0:T(512)S(1)} %get-tuple-element.19, f32[272]{0:T(512)S(1)} %copy-done.68, f32[272]{0:T(512)S(1)} %copy-done.69), channel_id=1, replica_groups=mesh['row'=32,'col'=4] {'row'}, use_global_device_ids=true, to_apply=%region_30.31 | all-reduce | flops 1088 | bytes 8704 | tf_op jit(solution)/shard_map/psum | solution.py:255
  1366.5 37.9 %all-reduce.9 = (f32[512]{0:T(512)S(1)}, f32[512]{0:T(512)S(1)}) all-reduce(f32[512]{0:T(512)S(1)} %get-tuple-element.13, f32[512]{0:T(512)S(1)} %get-tuple-element.16), channel_id=1, replica_groups=mesh['row'=32,'col'=4] {'col'}, use_global_device_ids=true, to_apply=%region_28.29 | all-reduce | flops 1024 | bytes 8192 | tf_op jit(solution)/shard_map/psum | solution.py:39
  (359 shorter events, 269.5 us)
Async XLA Ops:
  7.2 77.3 %all-gather.23.cloned.1.call-start = ((), (), s32[]{:S(2)}) async-start(), calls=%async_computation.18 | async-start | bytes 2365440 | tf_op jit(solution)/shard_map/all_gather | solution.py:104
  7.9 98.7 %all-gather.13.cloned.1.call-start = ((), (), s32[]{:S(2)}) async-start(), calls=%async_computation.9 | async-start | bytes 1392640 | tf_op jit(solution)/shard_map/all_gather | solution.py:43
  17.3 138.7 %all-gather.15.cloned.1.call-start = ((), (), s32[]{:S(2)}) async-start(), calls=%async_computation.10 | async-start | bytes 2785280 | tf_op jit(solution)/shard_map/all_gather | solution.py:119
  156.0 51.0 %collective-permute-start = (bf16[512,2176]{0,1:T(8,128)(2,1)}, bf16[512,2176]{0,1:T(8,128)(2,1)}, u32[]{:S(2)}, u32[]{:S(2)}) collective-permute-start(bf16[512,2176]{0,1:T(8,128)(2,1)} %all-gather.15.cloned.1.call-done), channel_id=1, source_target_pairs={{0,4},{4,8},{8,12},{12,16},{16,20},{20,24},{24,28},{28,32},{32,36}... | collective-permute-start | bytes 6684680 | tf_op jit(solution)/shard_map/ppermute | solution.py:22
  207.0 51.8 %collective-permute-start.1 = (bf16[512,2176]{0,1:T(8,128)(2,1)}, bf16[512,2176]{0,1:T(8,128)(2,1)}, u32[]{:S(2)}, u32[]{:S(2)}) collective-permute-start(bf16[512,2176]{0,1:T(8,128)(2,1)} %collective-permute-done), channel_id=1, source_target_pairs={{0,4},{4,8},{8,12},{12,16},{16,20},{20,24},{24,28},{28,32},{32,36}... | collective-permute-start | bytes 6684680 | tf_op jit(solution)/shard_map/ppermute | solution.py:22
  258.9 51.2 %collective-permute-start.2 = (bf16[512,2176]{0,1:T(8,128)(2,1)}, bf16[512,2176]{0,1:T(8,128)(2,1)S(1)}, u32[]{:S(2)}, u32[]{:S(2)}) collective-permute-start(bf16[512,2176]{0,1:T(8,128)(2,1)} %collective-permute-done.1), channel_id=1, source_target_pairs={{0,4},{4,8},{8,12},{12,16},{16,20},{20,24},{24,28},{28,32},{32,36}... | collective-permute-start | bytes 6684680 | tf_op jit(solution)/shard_map/ppermute | solution.py:22
  330.2 99.4 %all-to-all-start.1 = ((bf16[128,4,272]{0,2,1:T(8,128)(2,1)}), bf16[128,4,272]{0,2,1:T(8,128)(2,1)S(1)}, u32[]{:S(2)}, u32[]{:S(2)}) async-start(bf16[128,4,272]{0,2,1:T(8,128)(2,1)} %bitcast.16), calls=%async_computation.1 | async-start | bytes 557056 | tf_op jit(solution)/shard_map/all_to_all | solution.py:57
  335.5 139.7 %reduce-scatter.16.cloned.1.call-start = ((), (), s32[]{:S(2)}) async-start(), calls=%async_computation.11 | async-start | bytes 1392640 | tf_op jit(solution)/shard_map/reduce_scatter | solution.py:47
  432.7 119.6 %all-gather.25.cloned.1.call-start = ((), (), s32[]{:S(2)}) async-start(), calls=%async_computation.19 | async-start | bytes 3041280 | tf_op jit(solution)/shard_map/all_gather | solution.py:105
  433.3 193.7 %all-gather.27.cloned.1.call-start = ((), (), s32[]{:S(2)}) async-start(), calls=%async_computation.20 | async-start | bytes 3041280 | tf_op jit(solution)/shard_map/all_gather | solution.py:107
  433.9 215.2 %all-gather.17.cloned.1.call-start = ((), (), s32[]{:S(2)}) async-start(), calls=%async_computation.12 | async-start | bytes 1392640 | tf_op jit(solution)/shard_map/all_gather | solution.py:43
  483.5 189.3 %all-gather.19.cloned.1.call-start = ((), (), s32[]{:S(2)}) async-start(), calls=%async_computation.14 | async-start | bytes 1392640 | tf_op jit(solution)/shard_map/all_gather | solution.py:43
  484.2 219.4 %reduce-scatter.20.cloned.1.call-start = ((), (), s32[]{:S(2)}) async-start(), calls=%async_computation.15 | async-start | bytes 1392640 | tf_op jit(solution)/shard_map/reduce_scatter | solution.py:47
  682.1 54.1 %all-gather.21.cloned.1.call-start = ((), (), s32[]{:S(2)}) async-start(), calls=%async_computation.16 | async-start | bytes 1392640 | tf_op jit(solution)/shard_map/all_gather | solution.py:43
  713.0 242.8 %reduce-scatter.24.cloned.1.call-start = ((), (), s32[]{:S(2)}) async-start(), calls=%async_computation.21 | async-start | bytes 2785280
  751.0 51.7 %collective-permute-start.3 = (bf16[512,2176]{0,1:T(8,128)(2,1)S(1)}, bf16[512,2176]{0,1:T(8,128)(2,1)S(1)}, u32[]{:S(2)}, u32[]{:S(2)}) collective-permute-start(bf16[512,2176]{0,1:T(8,128)(2,1)S(1)} %pad_maximum_fusion), channel_id=1, source_target_pairs={{4,0},{8,4},{12,8},{16,12},{20,16},{24,20},{28,24},{32,28},{36,32}... | collective-permute-start | bytes 6684680 | tf_op jit(solution)/shard_map/ppermute | solution.py:22
  803.5 50.6 %collective-permute-start.4 = (bf16[512,2176]{0,1:T(8,128)(2,1)S(1)}, bf16[512,2176]{0,1:T(8,128)(2,1)S(1)}, u32[]{:S(2)}, u32[]{:S(2)}) collective-permute-start(bf16[512,2176]{0,1:T(8,128)(2,1)S(1)} %fusion.4), channel_id=1, source_target_pairs={{4,0},{8,4},{12,8},{16,12},{20,16},{24,20},{28,24},{32,28},{36,32}... | collective-permute-start | bytes 6684680 | tf_op jit(solution)/shard_map/ppermute | solution.py:22
  855.0 49.7 %collective-permute-start.5 = (bf16[512,2176]{0,1:T(8,128)(2,1)S(1)}, bf16[512,2176]{0,1:T(8,128)(2,1)S(1)}, u32[]{:S(2)}, u32[]{:S(2)}) collective-permute-start(bf16[512,2176]{0,1:T(8,128)(2,1)S(1)} %fusion.5), channel_id=1, source_target_pairs={{4,0},{8,4},{12,8},{16,12},{20,16},{24,20},{28,24},{32,28},{36,32}... | collective-permute-start | bytes 6684680 | tf_op jit(solution)/shard_map/ppermute | solution.py:22
  908.1 380.0 %reduce-scatter.22.cloned.1.call-start = ((), (), s32[]{:S(2)}) async-start(), calls=%async_computation.17 | async-start | bytes 1392640 | tf_op jit(solution)/shard_map/reduce_scatter | solution.py:47
  976.4 428.0 %reduce-scatter.18.cloned.1.call-start = ((), (), s32[]{:S(2)}) async-start(), calls=%async_computation.13 | async-start | bytes 1392640 | tf_op jit(solution)/shard_map/reduce_scatter | solution.py:47
  1123.0 35.5 %collective-permute-start.16 = (bf16[272,48]{0,1:T(8,128)(2,1)}, bf16[272,48]{0,1:T(8,128)(2,1)S(1)}, u32[]{:S(2)}, u32[]{:S(2)}) collective-permute-start(bf16[272,48]{0,1:T(8,128)(2,1)} %get-tuple-element.39), channel_id=1, source_target_pairs={{0,4},{4,8},{8,12},{12,16},{16,20},{20,24},{24,28},{28,32},{32,36}... | collective-permute-start | bytes 78344
  1124.4 37.8 %collective-permute-start.17 = (bf16[272,48]{0,1:T(8,128)(2,1)}, bf16[272,48]{0,1:T(8,128)(2,1)S(1)}, u32[]{:S(2)}, u32[]{:S(2)}) collective-permute-start(bf16[272,48]{0,1:T(8,128)(2,1)} %get-tuple-element.39), channel_id=1, source_target_pairs={{0,8},{4,12},{8,16},{12,20},{16,24},{20,28},{24,32},{28,36},{32,40... | collective-permute-start | bytes 78344
  1125.7 41.1 %collective-permute-start.18 = (bf16[272,48]{0,1:T(8,128)(2,1)}, bf16[272,48]{0,1:T(8,128)(2,1)S(1)}, u32[]{:S(2)}, u32[]{:S(2)}) collective-permute-start(bf16[272,48]{0,1:T(8,128)(2,1)} %get-tuple-element.39), channel_id=1, source_target_pairs={{0,12},{4,16},{8,20},{12,24},{16,28},{20,32},{24,36},{28,40},{32,4... | collective-permute-start | bytes 78344
  1127.0 22.5 %collective-permute-start.15 = (bf16[2,816]{1,0:T(2,128)(2,1)S(1)}, bf16[2,816]{1,0:T(2,128)(2,1)S(1)}, u32[]{:S(2)}, u32[]{:S(2)}) collective-permute-start(bf16[2,816]{1,0:T(2,128)(2,1)S(1)} %slice.62), channel_id=1, source_target_pairs={{0,40},{4,44},{8,48},{12,52},{16,56},{20,60},{24,64},{28,68},{32,7... | collective-permute-start | bytes 9800
  1152.3 36.4 %collective-permute-start.10 = (bf16[48,816]{1,0:T(8,128)(2,1)S(1)}, bf16[48,816]{1,0:T(8,128)(2,1)S(1)}, u32[]{:S(2)}, u32[]{:S(2)}) collective-permute-start(bf16[48,816]{1,0:T(8,128)(2,1)S(1)} %get-tuple-element.38), channel_id=1, source_target_pairs={{0,20},{4,24},{8,28},{12,32},{16,36},{20,40},{24,44},{28,48},{32,5... | collective-permute-start | bytes 235016
  1153.6 37.1 %collective-permute-start.11 = (bf16[48,816]{1,0:T(8,128)(2,1)S(1)}, bf16[48,816]{1,0:T(8,128)(2,1)S(1)}, u32[]{:S(2)}, u32[]{:S(2)}) collective-permute-start(bf16[48,816]{1,0:T(8,128)(2,1)S(1)} %get-tuple-element.38), channel_id=1, source_target_pairs={{0,24},{4,28},{8,32},{12,36},{16,40},{20,44},{24,48},{28,52},{32,5... | collective-permute-start | bytes 235016
  1196.5 22.1 %collective-permute-start.37 = (bf16[1088,48]{0,1:T(8,128)(2,1)}, bf16[1088,48]{0,1:T(8,128)(2,1)S(1)}, u32[]{:S(2)}, u32[]{:S(2)}) collective-permute-start(bf16[1088,48]{0,1:T(8,128)(2,1)} %get-tuple-element.41), channel_id=1, source_target_pairs={{0,8},{4,12},{8,16},{12,20},{16,24},{20,28},{24,32},{28,36},{32,40... | collective-permute-start | bytes 313352
  1199.0 24.2 %collective-permute-start.38 = (bf16[1088,48]{0,1:T(8,128)(2,1)}, bf16[1088,48]{0,1:T(8,128)(2,1)S(1)}, u32[]{:S(2)}, u32[]{:S(2)}) collective-permute-start(bf16[1088,48]{0,1:T(8,128)(2,1)} %get-tuple-element.41), channel_id=1, source_target_pairs={{0,12},{4,16},{8,20},{12,24},{16,28},{20,32},{24,36},{28,40},{32,4... | collective-permute-start | bytes 313352
  1229.6 22.3 %collective-permute-start.44 = (bf16[1088,48]{0,1:T(8,128)(2,1)}, bf16[1088,48]{0,1:T(8,128)(2,1)S(1)}, u32[]{:S(2)}, u32[]{:S(2)}) collective-permute-start(bf16[1088,48]{0,1:T(8,128)(2,1)} %get-tuple-element.41), channel_id=1, source_target_pairs={{0,36},{4,40},{8,44},{12,48},{16,52},{20,56},{24,60},{28,64},{32,6... | collective-permute-start | bytes 313352
  1231.6 22.4 %collective-permute-start.26 = (bf16[48,1088]{1,0:T(8,128)(2,1)S(1)}, bf16[48,1088]{1,0:T(8,128)(2,1)S(1)}, u32[]{:S(2)}, u32[]{:S(2)}) collective-permute-start(bf16[48,1088]{1,0:T(8,128)(2,1)S(1)} %get-tuple-element.40), channel_id=1, source_target_pairs={{0,4},{4,8},{8,12},{12,16},{16,20},{20,24},{24,28},{28,32},{32,36}... | collective-permute-start | bytes 313352
  1234.7 21.8 %collective-permute-start.27 = (bf16[48,1088]{1,0:T(8,128)(2,1)S(1)}, bf16[48,1088]{1,0:T(8,128)(2,1)S(1)}, u32[]{:S(2)}, u32[]{:S(2)}) collective-permute-start(bf16[48,1088]{1,0:T(8,128)(2,1)S(1)} %get-tuple-element.40), channel_id=1, source_target_pairs={{0,8},{4,12},{8,16},{12,20},{16,24},{20,28},{24,32},{28,36},{32,40... | collective-permute-start | bytes 313352
  1239.4 21.3 %collective-permute-start.29 = (bf16[48,1088]{1,0:T(8,128)(2,1)S(1)}, bf16[48,1088]{1,0:T(8,128)(2,1)}, u32[]{:S(2)}, u32[]{:S(2)}) collective-permute-start(bf16[48,1088]{1,0:T(8,128)(2,1)S(1)} %get-tuple-element.40), channel_id=1, source_target_pairs={{0,16},{4,20},{8,24},{12,28},{16,32},{20,36},{24,40},{28,44},{32,4... | collective-permute-start | bytes 313352
  (104 other events, 1864.0 us)
Sparse Core Ops, SparseCore 0:
  11.1 73.3 all-gather.22
  86.7 19.8 all-gather.12
  124.5 31.4 all-gather.14
  432.8 42.2 reduce-scatter.15
  478.6 73.6 all-gather.24
  555.8 71.1 all-gather.26
  629.3 19.6 all-gather.16
  650.8 21.9 all-gather.18
  682.2 21.3 reduce-scatter.19
  713.1 22.9 all-gather.20
  908.2 47.5 reduce-scatter.23
  976.6 21.7 reduce-scatter.21
  1000.9 21.5 reduce-scatter.17
where the time goes:
time: 1420 us; the launch traced here: 1410 us
  waiting for transfers between devices  688 us (48%)
  blocking collectives  392 us (28%)
  starting transfers between devices  149 us (10%)
  local copies, waits for them, and re-layouts  76.2 us (5%)
  matrix products  60.6 us (4%)
  other arithmetic  31.5 us (2%)
  between operations  16.3 us (1%)
    ppermute x6, waiting for transfers between devices, from_behind(): return lax.ppermute(block, axis, route)  268 us
    unnamed x1, blocking collectives  131 us
    unnamed x41, starting transfers between devices  124 us
    all_gather x1, blocking collectives, per_device(): lax.all_gather(w_out, 'row', axis=1, tiled=True)  91.8 us
    all_gather x4, waiting for transfers between devices, spread_rows(): return lax.all_gather(piece, 'col', axis=1, tiled=True)  78.6 us
    psum x1, blocking collectives, per_device(): lax.psum((first_gain_portion, bias1_part, second_gain_portion, bias2_part...  77.1 us
    all_gather x1, waiting for transfers between devices, per_device(): lax.all_gather(w_down, 'row', axis=1, tiled=True)  70.2 us
    all_gather x1, waiting for transfers between devices, per_device(): lax.all_gather(w_up, 'row', axis=0, tiled=True)  68 us
  transfers between devices with their start and end apart: 60, of which 17 were waited for; matrix products, arithmetic and copies ran while one was open for 16% of the time, Pallas kernels for 0%

commit v1 on v0

v1 whole, which is shorter than its diff:
```python
import math

import jax
import jax.numpy as jnp
from jax import lax
from jax.experimental import pallas as pl
from jax.experimental.pallas import tpu as pltpu
from jax.sharding import PartitionSpec as P

HEADS = 17
HEAD_DIM = 64
D = 1088
SEQ = 2048
MAIN = 1024
WIDE = 1152
PACK = 1280
QKV_COLS = 816
QUARTER = 128
MSG = 384
KEYS = 512

gelu_coef = math.sqrt(2.0 / math.pi)
norm_epsilon = 1e-05
masked_score = -1e30
MESH = pl.DeviceIdType.MESH
F32 = jnp.float32
BF16 = jnp.bfloat16
VMEM_LIMIT = 60 * 1024 * 1024
ANY = pl.BlockSpec(memory_space=pl.ANY)

GATHER_ORDERS = (("x", "y", "z"), ("y", "z", "x"), ("z", "x", "y"))
SCATTER_ORDERS = (("z", "y", "x"), ("x", "z", "y"), ("y", "x", "z"))


def dot_nn(a, b):
    return lax.dot_general(a, b, (((1,), (0,)), ((), ())), preferred_element_type=F32)


def dot_nt(a, b):
    return lax.dot_general(a, b, (((1,), (1,)), ((), ())), preferred_element_type=F32)


class Place:
    def __init__(self):
        self.row = lax.axis_index("row")
        self.col = lax.axis_index("col")
        self.at = {
            "x": lax.rem(self.row, 4),
            "z": lax.rem(self.row // 4, 4),
            "y": (self.row // 16) * 2 + self.col // 2,
        }
        self.core = lax.rem(self.col, 2)

    def device(self, at, core):
        return ((at["y"] // 2) * 16 + at["z"] * 4 + at["x"], lax.rem(at["y"], 2) * 2 + core)

    def step(self, axis, distance):
        at = dict(self.at)
        at[axis] = lax.rem(at[axis] + distance + 4, 4)
        return self.device(at, self.core)

    def partner(self):
        return (self.row, self.col + 1 - 2 * self.core)

    def beside(self, distance):
        return (self.row, lax.rem(self.col + distance, 4))

    def neighbours(self):
        found = [self.step(axis, d) for axis in ("x", "y", "z") for d in (1, -1)]
        found.append(self.partner())
        other = lax.rem(self.col // 2 + 1, 2)
        found.append((self.row, other * 2 + 1 - self.core))
        return found


def greet(devices):
    barrier = pltpu.get_barrier_semaphore()
    for device in devices:
        pl.semaphore_signal(barrier, inc=1, device_id=device, device_id_type=MESH)
    pl.semaphore_wait(barrier, len(devices))


def everything():
    return slice(None)


def place_index(fixed):
    if "y" in fixed:
        y_lo, y_hi = lax.rem(fixed["y"], 2), fixed["y"] // 2
    else:
        y_lo, y_hi = everything(), everything()
    return (y_lo, y_hi, fixed.get("z", everything()), fixed.get("x", everything()))


def with_core(index, core):
    return (index[0], core) + tuple(index[1:])


def gather_kernel(
    block0, block1, block2, x_ref, g_ref, v_ref,
    all0, all1, all2, x_out, g_out, v_out,
    send, recv, local, core_send, core_recv, in_send, in_recv, in_local,
):
    me = Place()
    blocks = (block0, block1, block2)
    wholes = (all0, all1, all2)
    greet(me.neighbours())

    def region(piece, stage, value, rows=None):
        order = GATHER_ORDERS[piece]
        fixed = {order[stage]: value}
        for axis in order[stage + 1 :]:
            fixed[axis] = me.at[axis]
        index = with_core(place_index(fixed), me.core)
        if rows is not None:
            index = index + (pl.ds(rows, 16),)
        else:
            index = index + (everything(),)
        return wholes[piece].at[index]

    def remote(source, target, ssem, rsem, device):
        return pltpu.make_async_remote_copy(
            src_ref=source, dst_ref=target, send_sem=ssem, recv_sem=rsem,
            device_id=device, device_id_type=MESH,
        )

    sent = []

    pairs = ((x_ref, x_out), (g_ref, g_out))
    waits = []
    for n, (source, target) in enumerate(pairs):
        own = pltpu.make_async_copy(
            source.at[pl.ds(pl.multiple_of(me.col * QUARTER, QUARTER), QUARTER), :], target.at[me.col], in_local.at[n]
        )
        own.start()
        waits.append(own)
    own = pltpu.make_async_copy(v_ref, v_out.at[me.col], in_local.at[2])
    own.start()
    waits.append(own)
    arrivals = []

    own_copies = []
    for piece in range(3):
        copy = pltpu.make_async_copy(
            blocks[piece], region(piece, 0, me.at[GATHER_ORDERS[piece][0]]), local.at[piece]
        )
        copy.start()
        own_copies.append(copy)

    def begin(piece, stage):
        axis = GATHER_ORDERS[piece][stage]
        mine = region(piece, stage, me.at[axis])
        source = blocks[piece] if stage == 0 else mine
        for n, distance in enumerate((1, -1)):
            copy = remote(
                source, mine, send.at[piece, stage, n], recv.at[piece, stage, n], me.step(axis, distance)
            )
            copy.start()
            sent.append(copy)

    def arrived(piece, stage, n):
        axis = GATHER_ORDERS[piece][stage]
        value = lax.rem(me.at[axis] + (3, 1, 2, 2)[n], 4)
        rows = (None, None, 0, 16)[n]
        there = region(piece, stage, value, rows)
        remote(
            there, there, send.at[piece, stage, n], recv.at[piece, stage, n], me.step(axis, 1)
        ).wait_recv()
        return value

    def forward(piece, stage, n, value):
        axis = GATHER_ORDERS[piece][stage]
        part = region(piece, stage, value, (0, 16)[n])
        copy = remote(
            part, part, send.at[piece, stage, 2 + n], recv.at[piece, stage, 2 + n],
            me.step(axis, (1, -1)[n]),
        )
        copy.start()
        sent.append(copy)

    def share(piece, n, value, rows=None):
        part = region(piece, 2, value, rows)
        copy = remote(part, part, core_send.at[piece, n], core_recv.at[piece, n], me.partner())
        copy.start()
        sent.append(copy)

    for piece in range(3):
        begin(piece, 0)
    for distance in (1, 2, 3):
        peer = me.beside(distance)
        for n, (source, target) in enumerate(pairs):
            copy = remote(
                source.at[pl.ds(pl.multiple_of(peer[1] * QUARTER, QUARTER), QUARTER), :], target.at[me.col],
                in_send.at[n, distance - 1], in_recv.at[n, distance - 1], peer,
            )
            copy.start()
            sent.append(copy)
            arrivals.append(
                remote(
                    source.at[pl.ds(0, QUARTER), :], target.at[lax.rem(me.col + 4 - distance, 4)],
                    in_send.at[n, distance - 1], in_recv.at[n, distance - 1], peer,
                )
            )
        copy = remote(v_ref, v_out.at[me.col], in_send.at[2, distance - 1], in_recv.at[2, distance - 1], peer)
        copy.start()
        sent.append(copy)
        arrivals.append(
            remote(
                v_ref, v_out.at[lax.rem(me.col + 4 - distance, 4)],
                in_send.at[2, distance - 1], in_recv.at[2, distance - 1], peer,
            )
        )
    for copy in own_copies:
        copy.wait()
    for stage in range(3):
        if stage > 0:
            for piece in range(3):
                begin(piece, stage)
        if stage == 2:
            for piece in range(3):
                share(piece, 0, me.at[GATHER_ORDERS[piece][2]])
        for n in range(2):
            for piece in range(3):
                value = arrived(piece, stage, n)
                forward(piece, stage, n, value)
                if stage == 2:
                    share(piece, 1 + n, value)
        for n in (2, 3):
            for piece in range(3):
                value = arrived(piece, stage, n)
                if stage == 2:
                    share(piece, 1 + n, value, (0, 16)[n - 2])
    for piece in range(3):
        axis = GATHER_ORDERS[piece][2]
        fixed_rows = (None, None, None, 0, 16)
        for n, offset in enumerate((0, 3, 1, 2, 2)):
            value = lax.rem(me.at[axis] + offset, 4)
            index = with_core(place_index({axis: value}), 1 - me.core)
            rows = fixed_rows[n]
            index = index + ((everything(),) if rows is None else (pl.ds(rows, 16),))
            there = wholes[piece].at[index]
            remote(there, there, core_send.at[piece, n], core_recv.at[piece, n], me.partner()).wait_recv()
    for copy in arrivals:
        copy.wait_recv()
    for copy in waits:
        copy.wait()
    for copy in sent:
        copy.wait_send()


def gather_all(blocks, x, g, v):
    whole = jax.ShapeDtypeStruct((2, 2, 2, 4, 4, 32, PACK), BF16)
    quarter = jax.ShapeDtypeStruct((4, QUARTER, 272), BF16)
    return pl.pallas_call(
        gather_kernel,
        out_shape=(whole, whole, whole, quarter, quarter, jax.ShapeDtypeStruct((4, 8, 272), F32)),
        in_specs=[ANY] * 6,
        out_specs=(ANY,) * 6,
        scratch_shapes=[
            pltpu.SemaphoreType.DMA((3, 3, 4)),
            pltpu.SemaphoreType.DMA((3, 3, 4)),
            pltpu.SemaphoreType.DMA((3,)),
            pltpu.SemaphoreType.DMA((3, 5)),
            pltpu.SemaphoreType.DMA((3, 5)),
            pltpu.SemaphoreType.DMA((3, 3)),
            pltpu.SemaphoreType.DMA((3, 3)),
            pltpu.SemaphoreType.DMA((3,)),
        ],
        compiler_params=pltpu.CompilerParams(collective_id=0, has_side_effects=True),
        name="gather_weights",
    )(*blocks, x, g, v)


def exchange_kernel(source, target, send, recv, local):
    row, col = lax.axis_index("row"), lax.axis_index("col")
    in_group = lax.rem(row + 2, 4)
    rank = in_group * 4 + col

    def device(other):
        return (lax.rem(row - in_group + other // 4 + 32, 32), lax.rem(other, 4))

    greet([device(lax.rem(rank + d, 16)) for d in range(1, 16)])
    own = pltpu.make_async_copy(source.at[rank], target.at[rank], local)
    own.start()
    copies = []
    for d in range(1, 16):
        other = lax.rem(rank + d, 16)
        copy = pltpu.make_async_remote_copy(
            src_ref=source.at[other], dst_ref=target.at[rank], send_sem=send.at[d], recv_sem=recv.at[d],
            device_id=device(other), device_id_type=MESH,
        )
        copy.start()
        copies.append(copy)
    for d in range(1, 16):
        origin = lax.rem(rank + 16 - d, 16)
        pltpu.make_async_remote_copy(
            src_ref=source.at[origin], dst_ref=target.at[origin], send_sem=send.at[d], recv_sem=recv.at[d],
            device_id=device(origin), device_id_type=MESH,
        ).wait_recv()
    for copy in copies:
        copy.wait_send()
    own.wait()


def exchange(source, collective_id):
    return pl.pallas_call(
        exchange_kernel,
        out_shape=jax.ShapeDtypeStruct(source.shape, source.dtype),
        in_specs=[ANY],
        out_specs=ANY,
        scratch_shapes=[
            pltpu.SemaphoreType.DMA((16,)),
            pltpu.SemaphoreType.DMA((16,)),
            pltpu.SemaphoreType.DMA,
        ],
        compiler_params=pltpu.CompilerParams(collective_id=collective_id, has_side_effects=True),
        name="exchange_heads",
    )(source)


def free_axes(fixed):
    return [axis for axis in ("y", "z", "x") if axis not in fixed]


def buffer_shape(fixed, rows):
    shape = ()
    for axis in free_axes(fixed):
        shape = shape + ((2, 2) if axis == "y" else (4,))
    return shape + (rows, PACK)


def buffer_index(at):
    index = ()
    for axis in ("y", "z", "x"):
        if axis in at:
            index = index + ((lax.rem(at[axis], 2), at[axis] // 2) if axis == "y" else (at[axis],))
    return index


def scatter_kernel(part0, part1, part2, y_ref, gin_ref, out_ref, y_out, gin_out, *scratch):
    me = Place()
    parts = (part0, part1, part2)
    sums, others = scratch[0:3], scratch[3:6]
    halves = {}
    fulls = {}
    position = 6
    for piece in range(3):
        for stage in range(3):
            halves[piece, stage] = scratch[position : position + 2]
            fulls[piece, stage] = scratch[position + 2 : position + 4]
            position += 4
    local, core_send, core_recv, send, recv, out_send, out_recv, out_local = scratch[position:]
    greet(me.neighbours())

    def remote(source, target, ssem, rsem, device):
        return pltpu.make_async_remote_copy(
            src_ref=source, dst_ref=target, send_sem=ssem, recv_sem=rsem,
            device_id=device, device_id_type=MESH,
        )

    def chunk_value(piece, k):
        return lax.rem(me.at[SCATTER_ORDERS[piece][0]] + (2, 1, 3, 0)[k], 4)

    sent, loads, crossed = [], {}, {}
    for k in range(4):
        for piece in range(3):
            index = place_index({SCATTER_ORDERS[piece][0]: chunk_value(piece, k)})
            load = pltpu.make_async_copy(
                parts[piece].at[with_core(index, me.core)], sums[piece].at[index], local.at[piece, k]
            )
            load.start()
            loads[piece, k] = load
            copy = remote(
                parts[piece].at[with_core(index, 1 - me.core)], others[piece].at[index],
                core_send.at[piece, k], core_recv.at[piece, k], me.partner(),
            )
            copy.start()
            crossed[piece, k] = copy
            sent.append(copy)

    pairs = ((y_ref, y_out), (gin_ref, gin_out))
    arrivals, own_copies = [], []
    for n, (source, target) in enumerate(pairs):
        rows = pl.ds(pl.multiple_of(me.col * QUARTER, QUARTER), QUARTER)
        own = pltpu.make_async_copy(source.at[me.col], target.at[rows, :], out_local.at[n])
        own.start()
        own_copies.append(own)
        for distance in (1, 2, 3):
            peer = me.beside(distance)
            copy = remote(
                source.at[peer[1]], target.at[rows, :], out_send.at[n, distance - 1], out_recv.at[n, distance - 1], peer
            )
            copy.start()
            sent.append(copy)
            origin = pl.ds(pl.multiple_of(lax.rem(me.col + 4 - distance, 4) * QUARTER, QUARTER), QUARTER)
            arrivals.append(
                remote(
                    source.at[me.col], target.at[origin, :],
                    out_send.at[n, distance - 1], out_recv.at[n, distance - 1], peer,
                )
            )

    def stage_fixed(piece, stage):
        return {axis: me.at[axis] for axis in SCATTER_ORDERS[piece][:stage]}

    def each_tile(fixed, body):
        axes = free_axes(fixed)
        count = 4 ** len(axes)
        if count == 1:
            body({})
            return

        @pl.loop(0, count)
        def _(t):
            if len(axes) == 1:
                body({axes[0]: t})
            else:
                body({axes[0]: t // 4, axes[1]: lax.rem(t, 4)})

    def add_core(piece, k):
        axis = SCATTER_ORDERS[piece][0]
        fixed = {axis: chunk_value(piece, k)}

        def body(at):
            index = place_index({**fixed, **at})
            total = sums[piece][index].astype(F32) + others[piece][index].astype(F32)
            sums[piece][index] = total.astype(BF16)

        each_tile(fixed, body)

    def begin(piece, stage):
        axis = SCATTER_ORDERS[piece][stage]
        fixed = {**stage_fixed(piece, stage), axis: lax.rem(me.at[axis] + 2, 4)}
        for n in range(2):
            copy = remote(
                sums[piece].at[place_index(fixed) + (pl.ds(16 * n, 16),)], halves[piece, stage][n],
                send.at[piece, stage, n], recv.at[piece, stage, n], me.step(axis, (1, -1)[n]),
            )
            copy.start()
            sent.append(copy)

    def middle(piece, stage, n):
        axis = SCATTER_ORDERS[piece][stage]
        fixed = {**stage_fixed(piece, stage), axis: lax.rem(me.at[axis] + (1, 3)[n], 4)}
        part = halves[piece, stage][n]
        remote(part, part, send.at[piece, stage, n], recv.at[piece, stage, n], me.step(axis, 1)).wait_recv()

        def body(at):
            index = place_index({**fixed, **at}) + (pl.ds(16 * n, 16),)
            total = sums[piece][index].astype(F32) + part[buffer_index(at)].astype(F32)
            sums[piece][index] = total.astype(BF16)

        each_tile(fixed, body)
        copy = remote(
            sums[piece].at[place_index(fixed)], fulls[piece, stage][n],
            send.at[piece, stage, 2 + n], recv.at[piece, stage, 2 + n], me.step(axis, (1, -1)[n]),
        )
        copy.start()
        sent.append(copy)

    def finish(piece, stage):
        axis = SCATTER_ORDERS[piece][stage]
        fixed = {**stage_fixed(piece, stage), axis: me.at[axis]}
        first, second = fulls[piece, stage]
        for n, part in enumerate((first, second)):
            remote(
                part, part, send.at[piece, stage, 2 + n], recv.at[piece, stage, 2 + n], me.step(axis, 1)
            ).wait_recv()

        def body(at):
            index = place_index({**fixed, **at})
            place = buffer_index(at)
            if stage == 2:
                total = sums[piece][index].astype(F32) + (first[...].astype(F32) + second[...].astype(F32))
                out_ref[piece] = total
            else:
                total = sums[piece][index].astype(F32) + (first[place].astype(F32) + second[place].astype(F32))
                sums[piece][index] = total.astype(BF16)

        each_tile(fixed, body)

    for k in range(4):
        for piece in range(3):
            loads[piece, k].wait()
            crossed[piece, k].wait_recv()
            add_core(piece, k)
            if k == 0:
                begin(piece, 0)
            elif k < 3:
                middle(piece, 0, k - 1)
    for piece in range(3):
        finish(piece, 0)
        begin(piece, 1)
    for stage in (1, 2):
        for n in range(2):
            for piece in range(3):
                middle(piece, stage, n)
        for piece in range(3):
            finish(piece, stage)
            if stage == 1:
                begin(piece, 2)
    for copy in arrivals:
        copy.wait_recv()
    for copy in own_copies:
        copy.wait()
    for copy in sent:
        copy.wait_send()


def scatter_all(parts, y4, gin4):
    scratch = [pltpu.VMEM((2, 2, 4, 4, 32, PACK), BF16) for _ in range(6)]
    for piece in range(3):
        order = SCATTER_ORDERS[piece]
        for stage in range(3):
            fixed = order[: stage + 1]
            scratch += [pltpu.VMEM(buffer_shape(fixed, 16), BF16) for _ in range(2)]
            scratch += [pltpu.VMEM(buffer_shape(fixed, 32), BF16) for _ in range(2)]
    scratch += [
        pltpu.SemaphoreType.DMA((3, 4)),
        pltpu.SemaphoreType.DMA((3, 4)),
        pltpu.SemaphoreType.DMA((3, 4)),
        pltpu.SemaphoreType.DMA((3, 3, 4)),
        pltpu.SemaphoreType.DMA((3, 3, 4)),
        pltpu.SemaphoreType.DMA((2, 3)),
        pltpu.SemaphoreType.DMA((2, 3)),
        pltpu.SemaphoreType.DMA((2,)),
    ]
    back = jax.ShapeDtypeStruct((512, 272), BF16)
    return pl.pallas_call(
        scatter_kernel,
        out_shape=(jax.ShapeDtypeStruct((3, 32, PACK), F32), back, back),
        in_specs=[ANY] * 5,
        out_specs=(pl.BlockSpec(memory_space=pltpu.VMEM), ANY, ANY),
        scratch_shapes=scratch,
        compiler_params=pltpu.CompilerParams(
            collective_id=3, has_side_effects=True, vmem_limit_bytes=VMEM_LIMIT
        ),
        name="scatter_gradients",
    )(*parts, y4, gin4)


def unpack_tail(packed, tiles, wide, tail):
    tiles[...] = packed[0, :, WIDE:PACK].astype(F32)
    for j in range(2):
        for s in range(9):
            wide[pl.ds(32 * j, 32), pl.ds(128 * s, 128)] = tiles[pl.ds(9 * j + s, 32, stride=32), :]
    tail[0:64, :] = wide[0:64, :].astype(BF16)


def pack_tail(tail, tiles, packed):
    for j in range(2):
        for s in range(9):
            tiles[pl.ds(9 * j + s, 32, stride=32), :] = tail[32 * j : 32 * j + 32, 128 * s : 128 * s + 128]
    packed[0, :, WIDE:PACK] = tiles[...].astype(BF16)


def in_features(values, packed, tail, columns):
    return dot_nn(values[:, :MAIN], packed[0, :, columns]) + dot_nn(values[:, MAIN:], tail[:, columns])


def add_to_features(total, values, packed, tail):
    @pl.loop(0, 4)
    def _(b):
        rows = pl.ds(pl.multiple_of(b * 256, 256), 256)
        total[:, rows] += dot_nt(values, packed[0, rows, :WIDE])

    total[:, MAIN:] += dot_nt(values, tail[...])


def norm_forward(x, gain, bias):
    mean = jnp.sum(x, axis=1, keepdims=True) / D
    square = jnp.sum(x * x, axis=1, keepdims=True) / D
    inverse = lax.rsqrt(square - mean * mean + norm_epsilon)
    normed = (x - mean) * inverse
    return normed, inverse, (normed * gain + bias).astype(BF16)


def norm_reverse(grad, normed, inverse, gain):
    scaled = grad * gain
    first = jnp.sum(scaled, axis=1, keepdims=True) / D
    second = jnp.sum(scaled * normed, axis=1, keepdims=True) / D
    return inverse * (scaled - first - normed * second)


def permuted(pieces, perm):
    total = dot_nn(pieces[0], perm[0])
    for c in range(1, 4):
        total += dot_nn(pieces[c], perm[c])
    return total


def permuted_exact(pieces, perm):
    total = jnp.zeros((8, WIDE), F32)
    for c in range(4):
        total += lax.dot_general(
            pieces[c], perm[c].astype(F32), (((1,), (0,)), ((), ())),
            preferred_element_type=F32, precision=lax.Precision.HIGHEST,
        )
    return total


def real_features(values):
    lane = lax.broadcasted_iota(jnp.int32, values.shape, 1)
    return jnp.where(lane < D, values, 0.0)


def qkv_kernel(x4, v4, perm, packed, x_out, n1_out, v_out, qkv_out, tiles, wide, tail):
    @pl.when(pl.program_id(0) == 0)
    def _():
        x = permuted(x4, perm)
        vectors = permuted_exact(v4, perm)
        v_out[...] = vectors
        x_out[...] = x.astype(BF16)
        _, _, normed = norm_forward(x, vectors[0:1], vectors[1:2])
        n1_out[...] = normed
        tail[...] = jnp.zeros_like(tail)

    unpack_tail(packed, tiles, wide, tail)

    @pl.loop(0, 3)
    def _(b):
        columns = pl.ds(pl.multiple_of(b * 384, 128), 384)
        qkv_out[0, :, columns] = in_features(n1_out[...], packed, tail, columns).astype(BF16)


def whole_spec(shape):
    return pl.BlockSpec(shape, lambda s: (0,) * len(shape))


def qkv_call(x4, v4, perm, weights):
    row = jax.ShapeDtypeStruct((QUARTER, WIDE), BF16)
    return pl.pallas_call(
        qkv_kernel,
        grid=(4,),
        out_shape=(
            row, row, jax.ShapeDtypeStruct((8, WIDE), F32), jax.ShapeDtypeStruct((4, QUARTER, WIDE), BF16)
        ),
        in_specs=[
            whole_spec((4, QUARTER, 272)), whole_spec((4, 8, 272)), whole_spec((4, 272, WIDE)),
            pl.BlockSpec((1, MAIN, PACK), lambda s: (s, 0, 0)),
        ],
        out_specs=(
            whole_spec((QUARTER, WIDE)), whole_spec((QUARTER, WIDE)), whole_spec((8, WIDE)),
            pl.BlockSpec((1, QUARTER, WIDE), lambda s: (s, 0, 0)),
        ),
        scratch_shapes=[pltpu.VMEM((MAIN, 128), F32), pltpu.VMEM((128, WIDE), F32), pltpu.VMEM((128, WIDE), BF16)],
        compiler_params=pltpu.CompilerParams(vmem_limit_bytes=VMEM_LIMIT),
        name="norm_and_qkv",
    )(x4, v4, perm, weights)


def gelu_both(v):
    tanh_value = jnp.tanh(gelu_coef * (v + 0.044715 * v * v * v))
    value = 0.5 * v * (1.0 + tanh_value)
    slope = 0.5 * (1.0 + tanh_value) + 0.5 * v * (1.0 - tanh_value * tanh_value) * gelu_coef * (
        1.0 + 0.134145 * v * v
    )
    return value, slope


def weight_gradient(rows_t, values, tiles, tail_sum, packed):
    @pl.loop(0, 4)
    def _(b):
        rows = pl.ds(pl.multiple_of(b * 256, 256), 256)
        packed[0, rows, :WIDE] = dot_nn(rows_t[rows, :], values[...]).astype(BF16)

    tail_sum[...] = dot_nn(rows_t[MAIN:, :], values[...])
    pack_tail(tail_sum, tiles, packed)


def middle_kernel(
    x_ref, a0, w0, w1, w2, g4, perm, vec,
    y4, dres_out, dresb_out, gr1, gr2, dmix_out, vec_out,
    resid, normed2, n2, n2_t, cot, cot_t, total, dn2, inverse2, hidden, dpre, tiles, out_tiles, tail1, tail2, tail_sum,
):
    s = pl.program_id(0)

    @pl.when(s == 0)
    def _():
        total[...] = jnp.zeros_like(total)
        dn2[...] = jnp.zeros_like(dn2)
        tail1[...] = jnp.zeros_like(tail1)
        tail2[...] = jnp.zeros_like(tail2)
        out_tiles[...] = jnp.zeros_like(out_tiles)

    @pl.when((s < 4) | (s >= 8))
    def _():
        unpack_tail(w0, tiles, tail_sum, tail1)

    @pl.when(s < 4)
    def _():
        add_to_features(total, a0[0], w0, tail1)

    @pl.when(s == 3)
    def _():
        resid[...] = x_ref[...].astype(F32) + total[...]
        total[...] = jnp.zeros_like(total)
        normed, inverse, n2_value = norm_forward(resid[...], vec[2:3], vec[3:4])
        normed2[...] = normed
        inverse2[...] = jnp.broadcast_to(inverse, inverse2.shape)
        n2[...] = n2_value
        n2_t[...] = n2_value.astype(F32).T.astype(BF16)
        cot_value = permuted(g4, perm)
        cot[...] = cot_value.astype(BF16)
        cot_t[...] = cot_value.T.astype(BF16)

    @pl.when((s >= 4) & (s < 8))
    def _():
        unpack_tail(w1, tiles, tail_sum, tail1)
        unpack_tail(w2, tiles, tail_sum, tail2)

        @pl.loop(0, 3)
        def _(b):
            columns = pl.ds(pl.multiple_of(b * 384, 128), 384)
            pre = in_features(n2[...], w1, tail1, columns)
            d_hidden = in_features(cot[...], w2, tail2, columns)
            value, slope = gelu_both(pre)
            hidden[:, columns] = value.astype(BF16)
            dpre[:, columns] = (d_hidden * slope).astype(BF16)

        add_to_features(total, hidden[...], w2, tail2)
        add_to_features(dn2, dpre[...], w1, tail1)
        weight_gradient(n2_t, dpre, out_tiles, tail_sum, gr1)
        weight_gradient(cot_t, hidden, out_tiles, tail_sum, gr2)

    @pl.when(s == 7)
    def _():
        y = (resid[...] + total[...]).astype(BF16)
        for c in range(4):
            y4[c] = dot_nt(y, perm[c]).astype(BF16)
        grad = dn2[...]
        normed = normed2[...]
        vec_out[...] = jnp.zeros_like(vec_out)
        vec_out[0:1, :] = jnp.sum(grad * normed, axis=0, keepdims=True)
        vec_out[1:2, :] = jnp.sum(grad, axis=0, keepdims=True)
        back = cot[...].astype(F32) + norm_reverse(grad, normed, inverse2[:, 0:1], vec[2:3])
        back = real_features(back)
        dres_out[...] = back
        dresb_out[...] = back.astype(BF16)

    @pl.when(s >= 8)
    def _():
        @pl.loop(0, 3)
        def _(b):
            columns = pl.ds(pl.multiple_of(b * 384, 128), 384)
            dmix_out[0, :, columns] = in_features(dresb_out[...], w0, tail1, columns).astype(BF16)


def middle_call(x, a0, w0, w1, w2, g4, perm, vec):
    row_b = jax.ShapeDtypeStruct((QUARTER, WIDE), BF16)
    row_f = jax.ShapeDtypeStruct((QUARTER, WIDE), F32)
    packed = jax.ShapeDtypeStruct((4, MAIN, PACK), BF16)

    def early(s):
        return (jnp.minimum(s, 3), 0, 0)

    def outer(s):
        return (jnp.where(s < 8, jnp.minimum(s, 3), 11 - s), 0, 0)

    def inner(s):
        return (jnp.clip(s - 4, 0, 3), 0, 0)

    def late(s):
        return (jnp.where(s < 8, 3, 11 - s), 0, 0)

    block = (1, MAIN, PACK)
    rows = (1, QUARTER, WIDE)
    return pl.pallas_call(
        middle_kernel,
        grid=(12,),
        out_shape=(
            jax.ShapeDtypeStruct((4, QUARTER, 272), BF16), row_f, row_b, packed, packed,
            jax.ShapeDtypeStruct((4, QUARTER, WIDE), BF16), jax.ShapeDtypeStruct((8, WIDE), F32),
        ),
        in_specs=[
            whole_spec((QUARTER, WIDE)), pl.BlockSpec(rows, early), pl.BlockSpec(block, outer),
            pl.BlockSpec(block, inner), pl.BlockSpec(block, inner), whole_spec((4, QUARTER, 272)),
            whole_spec((4, 272, WIDE)), whole_spec((8, WIDE)),
        ],
        out_specs=(
            whole_spec((4, QUARTER, 272)), whole_spec((QUARTER, WIDE)), whole_spec((QUARTER, WIDE)),
            pl.BlockSpec(block, inner), pl.BlockSpec(block, inner), pl.BlockSpec(rows, late), whole_spec((8, WIDE)),
        ),
        scratch_shapes=[
            pltpu.VMEM((QUARTER, WIDE), F32), pltpu.VMEM((QUARTER, WIDE), F32), pltpu.VMEM((QUARTER, WIDE), BF16),
            pltpu.VMEM((WIDE, QUARTER), BF16), pltpu.VMEM((QUARTER, WIDE), BF16), pltpu.VMEM((WIDE, QUARTER), BF16),
            pltpu.VMEM((QUARTER, WIDE), F32), pltpu.VMEM((QUARTER, WIDE), F32), pltpu.VMEM((QUARTER, 128), F32),
            pltpu.VMEM((QUARTER, WIDE), BF16), pltpu.VMEM((QUARTER, WIDE), BF16),
            pltpu.VMEM((MAIN, 128), F32), pltpu.VMEM((MAIN, 128), F32),
            pltpu.VMEM((128, WIDE), BF16), pltpu.VMEM((128, WIDE), BF16), pltpu.VMEM((128, WIDE), F32),
        ],
        compiler_params=pltpu.CompilerParams(vmem_limit_bytes=VMEM_LIMIT),
        name="feed_forward",
    )(x, a0, w0, w1, w2, g4, perm, vec)


def first_kernel(
    x_ref, n1, dresb, dres, both, w0, perm, vec, vec2,
    gin4, gr0, sums,
    both_t, dn1, tiles, out_tiles, tail, tail_sum,
):
    s = pl.program_id(0)

    @pl.when(s == 0)
    def _():
        dn1[...] = jnp.zeros_like(dn1)
        tail[...] = jnp.zeros_like(tail)
        out_tiles[...] = jnp.zeros_like(out_tiles)
        both_t[:, 0:128] = n1[...].astype(F32).T.astype(BF16)
        both_t[:, 128:256] = dresb[...].astype(F32).T.astype(BF16)

    unpack_tail(w0, tiles, tail_sum, tail)
    add_to_features(dn1, both[0, 0:128, :], w0, tail)
    weight_gradient(both_t, both.at[0], out_tiles, tail_sum, gr0)

    @pl.when(s == 3)
    def _():
        normed, inverse, _ = norm_forward(x_ref[...].astype(F32), vec[0:1], vec[1:2])
        grad = dn1[...]
        back = dres[...] + norm_reverse(grad, normed, inverse, vec[0:1])
        back = real_features(back).astype(BF16)
        sums[...] = vec2[...]
        sums[4:5, :] = jnp.sum(grad * normed, axis=0, keepdims=True)
        sums[5:6, :] = jnp.sum(grad, axis=0, keepdims=True)
        for c in range(4):
            gin4[c] = dot_nt(back, perm[c]).astype(BF16)


def first_call(x, n1, dresb, dres, both, w0, perm, vec, vec2):
    block = (1, MAIN, PACK)

    def by_step(s):
        return (s, 0, 0)

    return pl.pallas_call(
        first_kernel,
        grid=(4,),
        out_shape=(
            jax.ShapeDtypeStruct((4, QUARTER, 272), BF16), jax.ShapeDtypeStruct((4, MAIN, PACK), BF16),
            jax.ShapeDtypeStruct((8, WIDE), F32),
        ),
        in_specs=[
            whole_spec((QUARTER, WIDE)), whole_spec((QUARTER, WIDE)), whole_spec((QUARTER, WIDE)),
            whole_spec((QUARTER, WIDE)), pl.BlockSpec((1, 256, WIDE), by_step),
            pl.BlockSpec(block, by_step), whole_spec((4, 272, WIDE)), whole_spec((8, WIDE)), whole_spec((8, WIDE)),
        ],
        out_specs=(whole_spec((4, QUARTER, 272)), pl.BlockSpec(block, by_step), whole_spec((8, WIDE))),
        scratch_shapes=[
            pltpu.VMEM((WIDE, 256), BF16), pltpu.VMEM((QUARTER, WIDE), F32),
            pltpu.VMEM((MAIN, 128), F32), pltpu.VMEM((MAIN, 128), F32), pltpu.VMEM((128, WIDE), BF16),
            pltpu.VMEM((128, WIDE), F32),
        ],
        compiler_params=pltpu.CompilerParams(vmem_limit_bytes=VMEM_LIMIT),
        name="first_norm_back",
    )(x, n1, dresb, dres, both, w0, perm, vec, vec2)


def allowed_pairs(shape, key_start, query_start):
    key = key_start + lax.broadcasted_iota(jnp.int32, shape, 0)
    query = query_start + lax.broadcasted_iota(jnp.int32, shape, 1)
    return key <= query


def transposed(values):
    return values.astype(F32).T


def attend_kernel(info, r_ref, q16, o_out, o16_out, l_out, l16_out, query, value_t, value16_t):
    rank, wraps = info[0], info[1]

    @pl.loop(0, 4)
    def _(b):
        rows = pl.ds(pl.multiple_of(b * KEYS, KEYS), KEYS)
        query[rows, :] = r_ref[rows, 0:64] * jnp.asarray(0.125, BF16)
        value_t[:, rows] = transposed(r_ref[rows, 128:256])[0:64].astype(BF16)
        value16_t[:, rows] = transposed(r_ref[rows, 256:384])[0:64].astype(BF16)

    def step(q, columns, v_t, j, carry, query_start=None):
        peak, running, mixed = carry
        rows = pl.ds(pl.multiple_of(j * KEYS, KEYS), KEYS)
        scores = dot_nt(r_ref[rows, columns], q)
        if query_start is not None:
            scores = jnp.where(allowed_pairs(scores.shape, j * KEYS, query_start), scores, masked_score)
        new_peak = jnp.maximum(peak, jnp.max(scores, axis=0, keepdims=True))
        shrink = jnp.exp(peak - new_peak)
        weights = jnp.exp(scores - new_peak)
        running = running * shrink + jnp.sum(weights, axis=0, keepdims=True)
        mixed = mixed * shrink + dot_nn(v_t[:, rows], weights.astype(BF16))
        return new_peak, running, mixed

    def empty(width):
        return (
            jnp.full((1, width), masked_score, F32), jnp.zeros((1, width), F32), jnp.zeros((64, width), F32)
        )

    @pl.loop(0, 4)
    def _(i):
        rows = pl.ds(pl.multiple_of(i * KEYS, KEYS), KEYS)
        q = query[rows, :]
        start = jnp.where((wraps == 1) & (i >= 2), 2, 0)
        carry = lax.fori_loop(
            start, i, lambda j, carry: step(q, slice(64, 128), value_t, j, carry), empty(KEYS)
        )
        peak, running, mixed = step(q, slice(64, 128), value_t, i, carry, i * KEYS)
        o_out[rows, :] = (mixed / running).T.astype(BF16)
        l_out[:, rows] = peak + jnp.log(running)

    q = q16[...] * jnp.asarray(0.125, BF16)
    start = jnp.where((wraps == 1) & (rank >= 8), 2, 0)
    peak, running, mixed = lax.fori_loop(
        start, rank // 4 + 1,
        lambda j, carry: step(q, slice(192, 256), value16_t, j, carry, rank * QUARTER), empty(QUARTER),
    )
    o16_out[...] = (mixed / running).T.astype(BF16)
    l16_out[...] = peak + jnp.log(running)


VMEM_SPEC = pl.BlockSpec(memory_space=pltpu.VMEM)
SMEM_SPEC = pl.BlockSpec(memory_space=pltpu.SMEM)


def attend_call(info, r, q16):
    return pl.pallas_call(
        attend_kernel,
        out_shape=(
            jax.ShapeDtypeStruct((SEQ, 64), BF16), jax.ShapeDtypeStruct((QUARTER, 64), BF16),
            jax.ShapeDtypeStruct((1, SEQ), F32), jax.ShapeDtypeStruct((1, QUARTER), F32),
        ),
        in_specs=[SMEM_SPEC, VMEM_SPEC, VMEM_SPEC],
        out_specs=(VMEM_SPEC,) * 4,
        scratch_shapes=[pltpu.VMEM((SEQ, 64), BF16), pltpu.VMEM((64, SEQ), BF16), pltpu.VMEM((64, SEQ), BF16)],
        compiler_params=pltpu.CompilerParams(vmem_limit_bytes=VMEM_LIMIT),
        name="attend_forward",
    )(info, r, q16)


def attend_back_kernel(
    info, r_ref, q16, o_ref, o16, do_ref, do16, l_ref, l16,
    msg, dq16_out, query, key_t, key16_t, delta, dq_t,
):
    rank, wraps = info[0], info[1]

    @pl.loop(0, 4)
    def _(b):
        rows = pl.ds(pl.multiple_of(b * KEYS, KEYS), KEYS)
        query[rows, :] = r_ref[rows, 0:64] * jnp.asarray(0.125, BF16)
        key_t[:, rows] = transposed(r_ref[rows, 0:128])[64:128].astype(BF16)
        key16_t[:, rows] = transposed(r_ref[rows, 128:256])[64:128].astype(BF16)
        product = do_ref[rows, :].astype(F32) * o_ref[rows, :].astype(F32)
        delta[:, rows] = jnp.sum(product.T, axis=0, keepdims=True)
        dq_t[:, rows] = jnp.zeros((64, KEYS), F32)

    def pair(keys, values, q, d_out, log_total, delta_row, mask):
        scores = dot_nt(keys, q)
        probs = jnp.exp(scores - log_total)
        if mask is not None:
            probs = jnp.where(mask(scores.shape), probs, 0.0)
        probs = probs.astype(BF16)
        d_prob = dot_nt(values, d_out)
        d_scores = (probs.astype(F32) * (d_prob - delta_row)).astype(BF16)
        return dot_nn(d_scores, q), dot_nn(probs, d_out), d_scores

    @pl.loop(0, 4)
    def _(j):
        rows = pl.ds(pl.multiple_of(j * KEYS, KEYS), KEYS)
        keys, values = r_ref[rows, 64:128], r_ref[rows, 128:192]

        def step(i, carry, mask=None):
            d_key, d_value = carry
            at = pl.ds(pl.multiple_of(i * KEYS, KEYS), KEYS)
            more_key, more_value, d_scores = pair(
                keys, values, query[at, :], do_ref[at, :], l_ref[:, at], delta[:, at], mask
            )
            dq_t[:, at] += dot_nn(key_t[:, rows], d_scores)
            return d_key + more_key, d_value + more_value

        zero = jnp.zeros((KEYS, 64), F32)
        carry = step(j, (zero, zero), lambda shape: allowed_pairs(shape, 0, 0))
        end = jnp.where((wraps == 1) & (j < 2), 2, 4)
        d_key, d_value = lax.fori_loop(j + 1, end, step, carry)
        msg[rows, 64:128] = d_key.astype(BF16)
        msg[rows, 128:192] = d_value.astype(BF16)

    q = q16[...] * jnp.asarray(0.125, BF16)
    d_out16 = do16[...]
    delta16 = jnp.sum((d_out16.astype(F32) * o16[...].astype(F32)).T, axis=0, keepdims=True)
    start = jnp.where((wraps == 1) & (rank >= 8), 2, 0)

    def last_step(j, dq):
        rows = pl.ds(pl.multiple_of(j * KEYS, KEYS), KEYS)
        d_key, d_value, d_scores = pair(
            r_ref[rows, 192:256], r_ref[rows, 256:320], q, d_out16, l16[...], delta16,
            lambda shape: allowed_pairs(shape, j * KEYS, rank * QUARTER),
        )
        msg[rows, 192:256] = d_key.astype(BF16)
        msg[rows, 256:320] = d_value.astype(BF16)
        return dq + dot_nn(key16_t[:, rows], d_scores)

    @pl.loop(0, 4)
    def _(j):
        rows = pl.ds(pl.multiple_of(j * KEYS, KEYS), KEYS)
        msg[rows, 192:256] = jnp.zeros((KEYS, 64), BF16)
        msg[rows, 256:384] = jnp.zeros((KEYS, 128), BF16)
        msg[rows, 0:64] = (dq_t[:, rows] * 0.125).T.astype(BF16)

    dq = lax.fori_loop(start, rank // 4 + 1, last_step, jnp.zeros((64, QUARTER), F32))
    dq16_out[...] = (dq * 0.125).T.astype(BF16)


def attend_back_call(info, r, q16, o, o16, do, do16, log_total, log16):
    return pl.pallas_call(
        attend_back_kernel,
        out_shape=(jax.ShapeDtypeStruct((SEQ, MSG), BF16), jax.ShapeDtypeStruct((QUARTER, 64), BF16)),
        in_specs=[SMEM_SPEC] + [VMEM_SPEC] * 8,
        out_specs=(VMEM_SPEC,) * 2,
        scratch_shapes=[
            pltpu.VMEM((SEQ, 64), BF16), pltpu.VMEM((64, SEQ), BF16), pltpu.VMEM((64, SEQ), BF16),
            pltpu.VMEM((1, SEQ), F32), pltpu.VMEM((64, SEQ), F32),
        ],
        compiler_params=pltpu.CompilerParams(vmem_limit_bytes=VMEM_LIMIT),
        name="attend_backward",
    )(info, r, q16, o, o16, do, do16, log_total, log16)


def packed_block(block):
    tail = jnp.pad(block[32:34], ((0, 0), (0, WIDE - D))).reshape(18, 128)
    return jnp.concatenate(
        [jnp.pad(block[:32], ((0, 0), (0, WIDE - D))), jnp.pad(tail, ((0, 14), (0, 0)))], axis=1
    )


def unpacked_block(packed):
    tail = packed[:18, WIDE:].reshape(2, WIDE)[:, :D]
    return jnp.concatenate([packed[:, :D], tail], axis=0)


def permutation():
    feature = jnp.arange(D, dtype=jnp.int32)
    block, inside = feature // 34, feature % 34
    place = jnp.where(inside < 32, 32 * block + inside, MAIN + 32 * (inside - 32) + block)
    chosen = place[:, None] == jnp.arange(WIDE, dtype=jnp.int32)[None, :]
    return chosen.astype(BF16).reshape(4, 272, WIDE)


def per_device(
    layer_input,
    first_norm_gain,
    first_norm_bias,
    w_qkv,
    w_out,
    second_norm_gain,
    second_norm_bias,
    w_up,
    w_down,
    gradient_of_output,
):
    row, col = lax.axis_index("row"), lax.axis_index("col")
    rank = (row + 2) % 4 * 4 + col
    wraps = ((row < 2) | (row >= 30)).astype(jnp.int32)
    info = jnp.stack([rank, wraps]).astype(jnp.int32)
    perm = permutation()
    vectors = jnp.concatenate(
        [
            jnp.stack([first_norm_gain, first_norm_bias, second_norm_gain, second_norm_bias]),
            jnp.zeros((4, 272), F32),
        ]
    )
    blocks = (
        packed_block(jnp.concatenate([w_qkv, w_out.T], axis=1)),
        packed_block(w_up),
        packed_block(w_down.T),
    )
    w0, w1, w2, x4, g4, v4 = gather_all(blocks, layer_input, gradient_of_output, vectors)
    w0, w1, w2 = (w.reshape(4, MAIN, PACK) for w in (w0, w1, w2))
    x, n1, vec, qkv4 = qkv_call(x4, v4, perm, w0)

    qkv = jnp.concatenate([qkv4[c, :, :QKV_COLS] for c in range(4)], axis=1).reshape(QUARTER, 3, HEADS, HEAD_DIM)
    last = [jnp.broadcast_to(qkv[:, n, 16:17], (QUARTER, 16, HEAD_DIM)) for n in (1, 2)]
    message = jnp.concatenate(
        [qkv[:, 0, :16], qkv[:, 1, :16], qkv[:, 2, :16], *last, jnp.zeros((QUARTER, 16, 64), BF16)], axis=2
    ).transpose(1, 0, 2)
    q16 = qkv[:, 0, 16]
    heads = exchange(message, 1).reshape(SEQ, MSG)
    o, o16, log_total, log16 = attend_call(info, heads, q16)
    mixed = exchange(o.reshape(16, QUARTER, 64), 2)
    attn = jnp.concatenate([mixed.transpose(1, 0, 2).reshape(QUARTER, 1024), o16], axis=1)
    a0 = jnp.pad(
        attn.reshape(QUARTER, 4, 272).transpose(1, 0, 2), ((0, 0), (0, 0), (QKV_COLS, WIDE - D))
    )
    y4, dres, dresb, gr1, gr2, dmix4, vec2 = middle_call(x, a0, w0, w1, w2, g4, perm, vec)
    dmix = jnp.concatenate([dmix4[c, :, QKV_COLS:D] for c in range(4)], axis=1).reshape(QUARTER, HEADS, HEAD_DIM)
    do = exchange(dmix[:, :16].transpose(1, 0, 2), 2).reshape(SEQ, 64)
    back, dq16 = attend_back_call(info, heads, q16, o, o16, do, dmix[:, 16], log_total, log16)
    back = exchange(back.reshape(16, QUARTER, MSG), 1)
    last_sums = jnp.sum(back[:, :, 192:320].astype(F32), axis=0).astype(BF16)

    def side_by_side(first, last_head):
        return jnp.concatenate(
            [back[:, :, first : first + 64].transpose(1, 0, 2).reshape(QUARTER, 1024), last_head], axis=1
        )

    d_qkv = jnp.concatenate(
        [side_by_side(0, dq16), side_by_side(64, last_sums[:, :64]), side_by_side(128, last_sums[:, 64:])], axis=1
    )
    dq0 = jnp.pad(
        d_qkv.reshape(QUARTER, 4, QKV_COLS).transpose(1, 0, 2), ((0, 0), (0, 0), (0, WIDE - QKV_COLS))
    )
    gin4, gr0, sums4 = first_call(
        x, n1, dresb, dres, jnp.concatenate([dq0, a0], axis=1), w0, perm, vec, vec2
    )
    grouped = tuple(g.reshape(2, 2, 2, 4, 4, 32, PACK) for g in (gr0, gr1, gr2))
    sums, layer_output, gin = scatter_all(grouped, y4, gin4)
    own_perm = lax.dynamic_index_in_dim(perm, col, 0, keepdims=False).astype(F32)
    vg = lax.dot_general(
        lax.psum(sums4, ("row", "col")), own_perm, (((1,), (1,)), ((), ())),
        preferred_element_type=F32, precision=lax.Precision.HIGHEST,
    )
    s0, s1, s2 = (unpacked_block(sums[n]) for n in range(3))
    return (
        layer_output,
        gin.astype(F32),
        vg[4],
        vg[5],
        s0[:, :QKV_COLS],
        s0[:, QKV_COLS:].T,
        vg[0],
        vg[1],
        s1,
        s2.T,
    )


def solution(mesh):
    placed = (
        P("row", "col"),
        P("col"),
        P("col"),
        P("row", "col"),
        P("col", "row"),
        P("col"),
        P("col"),
        P("row", "col"),
        P("col", "row"),
        P("row", "col"),
    )
    return jax.shard_map(
        per_device,
        mesh=mesh,
        in_specs=placed,
        out_specs=(
            P("row", "col"),
            P("row", "col"),
            P("col"),
            P("col"),
            P("row", "col"),
            P("col", "row"),
            P("col"),
            P("col"),
            P("row", "col"),
            P("col", "row"),
        ),
        check_vma=False,
    )
```

time: 1420 us -> 508 us (0.36)
  waiting for transfers between devices: 688 us -> 0 us
  Pallas kernels: 0 us -> 390 us
  blocking collectives: 392 us -> 67.3 us
  starting transfers between devices: 149 us -> 0 us
  matrix products: 60.6 us -> 1.55 us
  local copies, waits for them, and re-layouts: 76.2 us -> 35.2 us
  other arithmetic: 31.5 us -> 12.3 us
  between operations: 16.3 us -> 1.07 us
    pallas_call x0 -> x11, Pallas kernels: none -> 390 us  [the longest x4 94.5 us: exchange(): pl.pallas_call(exchange_kernel, out_shape=jax.ShapeDtypeStruct(source.sha...]
    all_gather x8 -> x0, waiting for transfers between devices: 315 us -> none  [the longest x4 78.6 us: spread_rows(): return lax.all_gather(piece, 'col', axis=1, tiled=True)]
    ppermute x6 -> x0, waiting for transfers between devices: 268 us -> none  [from_behind(): return lax.ppermute(block, axis, route)]
    unnamed x1 -> x0, blocking collectives: 131 us -> none
    unnamed x41 -> x0, starting transfers between devices: 124 us -> none
    all_gather x1 -> x0, blocking collectives: 91.8 us -> none  [per_device(): lax.all_gather(w_out, 'row', axis=1, tiled=True)]
    psum x5 -> x1, blocking collectives: 132 us -> 67.3 us  [per_device(): lax.psum(sums4, ('row', 'col'))]
    reduce_scatter x4 -> x0, waiting for transfers between devices: 62.7 us -> none  [feature_total(): lax.psum_scatter(partial_value.astype(jnp.bfloat16), 'col', scatter_dimen...]
  transfers between devices with their start and end apart: 60 -> 0, of which waited for: 17 -> 0; matrix products, arithmetic and copies ran while one was open for 16% -> 0% of each run, Pallas kernels for 0% -> 0%
where the time goes in v1:
time: 508 us; the launch traced here: 507 us
  Pallas kernels  390 us (77%)
  blocking collectives  67.3 us (13%)
  local copies, waits for them, and re-layouts  35.2 us (7%)
  other arithmetic  12.3 us (2%)
    pallas_call x4, Pallas kernels, exchange(): pl.pallas_call(exchange_kernel, out_shape=jax.ShapeDtypeStruct(source.sha...  94.5 us
    pallas_call x1, Pallas kernels, scatter_all(): pl.pallas_call(scatter_kernel, out_shape=(jax.ShapeDtypeStruct((3, 32, PA...  93.7 us
    pallas_call x1, Pallas kernels, gather_all(): pl.pallas_call(gather_kernel, out_shape=(whole, whole, whole, quarter, qu...  91.2 us
    psum x1, blocking collectives, per_device(): lax.psum(sums4, ('row', 'col'))  67.3 us
    pallas_call x1, Pallas kernels, middle_call(): pl.pallas_call(middle_kernel, grid=(12,), out_shape=(jax.ShapeDtypeStruct...  57.5 us
    pallas_call x1, Pallas kernels, first_call(): pl.pallas_call(first_kernel, grid=(4,), out_shape=(jax.ShapeDtypeStruct((...  21.1 us
    pallas_call x1, Pallas kernels, qkv_call(): pl.pallas_call(qkv_kernel, grid=(4,), out_shape=(row, row, jax.ShapeDtype...  12.4 us
    pallas_call x1, Pallas kernels, attend_back_call(): pl.pallas_call(attend_back_kernel, out_shape=(jax.ShapeDtypeStruct((SEQ,...  11.2 us

profile of v1, /device:TPU:1, one launch (start us, length us, event | category | flops | bytes accessed | tf_op | source)
XLA Modules:
  0.0 507.0 jit_solution(7018601340238505150)
XLA Ops:
  7.0 0.9 fusion.16
  7.9 0.9 slice.186
  9.4 0.9 slice.140
  11.0 1.9 copy.46.x_ref
  12.9 1.9 copy.47.g_ref
  14.8 2.8 iota_compare_fusion
  17.6 91.2 %gather_weights.1 = (bf16[2,2,2,4,4,32,1280]{6,5,4,3,2,1,0:T(8,128)(2,1)}, bf16[2,2,2,4,4,32,1280]{6,5,4,3,2,1,0:T(8,128)(2,1)}, bf16[2,2,2,4,4,32,1280]{6,5,4,3...) custom-call(bf16[32,1280]{1,0:T(8,128)(2,1)} %get-tuple-element.126.block0, ...), custom_call_target="tpu_custom_call" | custom-call | tf_op jit(solution)/shard_map/gather_weights/pallas_call | solution.py:254
  108.8 12.4 %norm_and_qkv.1 = (bf16[128,1152]{1,0:T(8,128)(2,1)}, bf16[128,1152]{1,0:T(8,128)(2,1)}, f32[8,1152]{1,0:T(8,128)}, bf16[4,128,1152]{2,1,0:T(8,128)(2,1)}) custom-call(bf16[4,128,272]{2,1,0:T(8,128)(2,1)} %get-tuple-element.39.x4, f32[4,8,272]{2,1,0:T(8,128)} %get-tuple-element.40.v4, bf16[4,272,1152]{2,1,0:T(8,128)(2,1)} %get-tuple-element.125.perm, ...), custom_call_target="tpu_custom_call" | custom-call | tf_op jit(solution)/shard_map/norm_and_qkv/pallas_call | solution.py:632
  121.2 1.4 slice_bitcast_fusion.3
  126.2 4.6 concatenate.48
  130.8 27.7 %exchange_heads.4 = bf16[16,128,384]{2,1,0:T(8,128)(2,1)} custom-call(bf16[16,128,384]{2,1,0:T(8,128)(2,1)} %bitcast.85), custom_call_target="tpu_custom_call" | custom-call | tf_op jit(solution)/shard_map/exchange_heads/pallas_call | solution.py:306
  158.5 8.0 %attend_forward.1 = (bf16[2048,64]{1,0:T(8,128)(2,1)}, bf16[128,64]{1,0:T(8,128)(2,1)}, f32[1,2048]{1,0:T(1,128)}, f32[1,128]{1,0:T(1,128)}) custom-call(s32[2]{0:T(128)} %pad_add_fusion.info, bf16[2048,384]{1,0:T(8,128)(2,1)} %bitcast.78, bf16[128,64]{1,0:T(8,128)(2,1)} %bitcast.106), custom_call_target="tpu_custom_call" | custom-call | tf_op jit(solution)/shard_map/attend_forward/pallas_call | solution.py:923
  166.5 0.8 copy.56
  167.3 23.0 %exchange_heads.5 = bf16[16,128,64]{2,1,0:T(8,128)(2,1)} custom-call(bf16[16,128,64]{2,1,0:T(8,128)(2,1)} %bitcast.89), custom_call_target="tpu_custom_call" | custom-call | tf_op jit(solution)/shard_map/exchange_heads/pallas_call | solution.py:306
  190.3 1.3 copy.55
  191.8 1.3 pad.47.a0
  193.1 57.5 %feed_forward.1 = (bf16[4,128,272]{2,1,0:T(8,128)(2,1)}, f32[128,1152]{1,0:T(8,128)}, bf16[128,1152]{1,0:T(8,128)(2,1)}, bf16[4,1024,1280]{2,1,0:T(8,128)(2,1)},...) custom-call(bf16[128,1152]{1,0:T(8,128)(2,1)} %get-tuple-element.42.x_ref, ...), custom_call_target="tpu_custom_call" | custom-call | tf_op jit(solution)/shard_map/feed_forward/pallas_call | solution.py:768
  250.6 1.2 slice_bitcast_fusion.10
  253.0 1.0 copy.74
  254.1 15.4 %exchange_heads.6 = bf16[16,128,64]{2,1,0:T(8,128)(2,1)} custom-call(bf16[16,128,64]{2,1,0:T(8,128)(2,1)} %bitcast.94), custom_call_target="tpu_custom_call" | custom-call | tf_op jit(solution)/shard_map/exchange_heads/pallas_call | solution.py:306
  269.5 11.2 %attend_backward.1 = (bf16[2048,384]{1,0:T(8,128)(2,1)}, bf16[128,64]{1,0:T(8,128)(2,1)}) custom-call(s32[2]{0:T(128)} %pad_add_fusion.info, bf16[2048,384]{1,0:T(8,128)(2,1)} %bitcast.79, bf16[128,64]{1,0:T(8,128)(2,1)} %bitcast.107, bf16[2048,64]{1,0:T(8,128)(2,1)} %get-tuple-element.45.o_ref, bf16[128,64]{1,0:T(8,128)(2,1)} %get-tuple-element.46.o16, ...), custom_call_target="tpu_custom_call" | custom-call | tf_op jit(solution)/shard_map/attend_backward/pallas_call | solution.py:1011
  280.7 28.4 %exchange_heads.7 = bf16[16,128,384]{2,1,0:T(8,128)(2,1)} custom-call(bf16[16,128,384]{2,1,0:T(8,128)(2,1)} %bitcast.96), custom_call_target="tpu_custom_call" | custom-call | tf_op jit(solution)/shard_map/exchange_heads/pallas_call | solution.py:306
  309.2 1.5 slice_reduce_fusion
  310.6 1.7 slice_bitcast_fusion
  314.1 1.6 fusion.1.both
  315.8 21.1 %first_norm_back.1 = (bf16[4,128,272]{2,1,0:T(8,128)(2,1)}, bf16[4,1024,1280]{2,1,0:T(8,128)(2,1)}, f32[8,1152]{1,0:T(8,128)}) custom-call(bf16[128,1152]{1,0:T(8,128)(2,1)} %get-tuple-element.42.x_ref, bf16[128,1152]{1,0:T(8,128)(2,1)} %get-tuple-element.43.n1, bf16[128,1152]{1,0:T(8,128)(2,1)} %get-tuple-element.51.dresb, ...), custom_call_target="tpu_custom_call" | custom-call | tf_op jit(solution)/shard_map/first_norm_back/pallas_call | solution.py:835
  336.9 93.7 %scatter_gradients.1 = (f32[3,32,1280]{2,1,0:T(8,128)}, bf16[512,272]{1,0:T(8,128)(2,1)}, bf16[512,272]{1,0:T(8,128)(2,1)}) custom-call(bf16[2,2,2,4,4,32,1280]{6,5,4,3,2,1,0:T(8,128)(2,1)} %bitcast.82, bf16[2,2,2,4,4,32,1280]{6,5,4,3,2,1,0:T(8,128)(2,1)} %bitcast.80, bf16[2,2,2,4,4,32,1280]{6,5,4,3,2,1,0:T(8,128)(2,1)} %bitcast.81, ...), custom_call_target="tpu_custom_call" | custom-call | tf_op jit(solution)/shard_map/scatter_gradients/pallas_call | solution.py:529
  430.6 1.9 copy.68
  432.5 67.3 %psum.7 = f32[8,1152]{1,0:T(8,128)S(1)} all-reduce(f32[8,1152]{1,0:T(8,128)S(1)} %copy-done.2), channel_id=1, replica_groups=mesh['row'=32,'col'=4] {'row','col'}, use_global_device_ids=true, to_apply=%region_1.2 | all-reduce | flops 9216 | bytes 73728 | tf_op jit(solution)/shard_map/psum | solution.py:1115
  499.8 1.5 fusion.2
  502.0 1.1 slice_bitcast_fusion.7
  506.0 1.0 copy.69
  (74 shorter events, 17.9 us)
Async XLA Ops:
  280.7 28.4 %copy-start.3 = (bf16[128,64]{1,0:T(8,128)(2,1)S(1)}, bf16[128,64]{1,0:T(8,128)(2,1)}, u32[]{:S(2)}) copy-start(bf16[128,64]{1,0:T(8,128)(2,1)} %get-tuple-element.57) | copy-start | bytes 49156
  312.8 1.3 copy-start
  336.8 95.7 %copy-start.2 = (f32[8,1152]{1,0:T(8,128)S(1)}, f32[8,1152]{1,0:T(8,128)}, u32[]{:S(2)}) copy-start(f32[8,1152]{1,0:T(8,128)} %get-tuple-element.66) | copy-start | bytes 110596
  430.6 75.4 %copy-start.1 = (bf16[512,272]{1,0:T(8,128)(2,1)S(1)}, bf16[512,272]{1,0:T(8,128)(2,1)}, u32[]{:S(2)}) copy-start(bf16[512,272]{1,0:T(8,128)(2,1)} %get-tuple-element.65) | copy-start | bytes 835588
